TPU v7x, 512 devices: a whole 4x4x16 slice. The times are simulated.
512 devices in a mesh: batch: 32 (over y_lo, z), seq: 16 (over y_hi, x, core).
Axes of the slice: x: 4, y: 4 (y_hi: 2, y_lo: 2; y = y_hi * 2 + y_lo), z: 16, core: 2. Of those that a mesh axis runs over, the one named last changes fastest.
Arguments:
- events: bfloat16 [32, 4096, 256], P('batch', 'seq'), may hold values from -6 to 6
- cotangent: bfloat16 [32, 4096, 256], P('batch', 'seq'), may hold values from -6 to 6
- bucket_ids: int32 [32, 4096, 128], P('batch', 'seq'), may hold values from 0 to 127
- history_lengths: int32 [32], P('batch'), may hold values from 256 to 4096, as said below
- w_in: bfloat16 [256, 1024], replicated, may hold values from -0.375 to 0.375
- b_in: float32 [1024], replicated, may hold values from -3 to 3
- w_out: bfloat16 [256, 256], replicated, may hold values from -0.375 to 0.375
- pos_table: float32 [4, 128], replicated, may hold values from -4 to 4
- time_table: float32 [4, 128], replicated, may hold values from -4 to 4
Outputs:
- layer_out: bfloat16 [32, 4096, 256], P('batch', 'seq')
- grad_events: bfloat16 [32, 4096, 256], P('batch', 'seq')
- grad_w_in: float32 [256, 1024], replicated
- grad_b_in: float32 [1024], replicated
- grad_w_out: float32 [256, 256], replicated
Inputs may be any that keep to these rules, and one draw needn't show every extreme that they name: `history_lengths`: each user has at least one slab of 256 real events; some user fills all 4096 positions and some user has exactly 256.
All inputs are finite; a program needn't handle non-finite values.
Results may differ from a plain program's by a relative error of at most 0.0064.
Values may be sent and summed in bfloat16 or wider, within the bound.
No kernel may reach another device: no remote copies, remote signals or barrier semaphores. Data moves between devices by JAX's collectives and lax.ppermute only.
A program may use at most 64 MiB of HBM per device.

v0:
```python
import math

import jax
import jax.numpy as jnp
from jax import lax
from jax.sharding import PartitionSpec as P

EPS = 1e-05


def from_behind(value, axis, steps):
    count = lax.axis_size(axis)
    leading, last = (max(0, -steps), min(count, count - steps))
    return lax.ppermute(value, axis, [(source, source + steps) for source in range(leading, last)])


def norm_rows(values):
    row_mean = jnp.mean(values, axis=-1, keepdims=True)
    centred = values - row_mean
    variance = jnp.mean(centred * centred, axis=-1, keepdims=True)
    inv_std = lax.rsqrt(variance + EPS)
    return (centred * inv_std, inv_std)


def norm_back(upstream, normed, inv_std):
    first = jnp.mean(upstream, axis=-1, keepdims=True)
    second = jnp.mean(upstream * normed, axis=-1, keepdims=True)
    return inv_std * (upstream - first - normed * second)


def silu_slope(pre_act):
    sigmoid = jax.nn.sigmoid(pre_act)
    return sigmoid * (1.0 + pre_act * (1.0 - sigmoid))


def skew_band(offset_bias):
    heads, window, _ = offset_bias.shape
    flipped = offset_bias[:, :, ::-1]
    padded = jnp.concatenate(
        [
            jnp.zeros((heads, window, 1), offset_bias.dtype),
            flipped,
            jnp.zeros((heads, window, window), offset_bias.dtype),
        ],
        axis=2,
    )
    flat = padded.reshape(heads, window * (2 * window + 1))[:, : window * 2 * window]
    return flat.reshape(heads, window, 2 * window)


def on_device(
    events, cotangent, bucket_ids, history_lengths, w_in, b_in, w_out, pos_table, time_table
):
    rows = events.shape[1]
    width = events.shape[2]
    heads, window = pos_table.shape
    head_size = width // heads
    blocks = rows // window
    f32 = jnp.float32
    user_events = events[0]
    user_cot = cotangent[0]
    user_ids = bucket_ids[0]
    length = history_lengths[0]
    base_pos = lax.axis_index("seq") * rows
    loss_scale = 1.0 / math.sqrt(lax.axis_size("batch") * lax.axis_size("seq") * rows)
    offsets = jnp.arange(window, dtype=jnp.int32)
    key_offsets = jnp.arange(2 * window, dtype=jnp.int32)
    ev_float = user_events.astype(f32)
    ev_hat, ev_inv = norm_rows(ev_float)
    ev_normed = ev_hat.astype(jnp.bfloat16)
    pre_act = jnp.dot(ev_normed, w_in, preferred_element_type=f32) + b_in
    projected = jax.nn.silu(pre_act).astype(jnp.bfloat16)
    gate_u = projected[:, :width]
    queries = projected[:, 2 * width : 3 * width]
    edge_keys, edge_values = from_behind(
        (projected[rows - window :, 3 * width :], projected[rows - window :, width : 2 * width]),
        "seq",
        1,
    )
    all_keys = jnp.concatenate([edge_keys, projected[:, 3 * width :]], axis=0)
    all_values = jnp.concatenate([edge_values, projected[:, width : 2 * width]], axis=0)

    def block_setup(block_index):
        begin_row = block_index * window
        q_rows = lax.dynamic_slice_in_dim(queries, begin_row, window, 0).reshape(
            window, heads, head_size
        )
        k_rows = lax.dynamic_slice_in_dim(all_keys, begin_row, 2 * window, 0).reshape(
            2 * window, heads, head_size
        )
        v_rows = lax.dynamic_slice_in_dim(all_values, begin_row, 2 * window, 0).reshape(
            2 * window, heads, head_size
        )
        id_rows = lax.dynamic_slice_in_dim(user_ids, begin_row, window, 0)
        query_pos = base_pos + begin_row + offsets
        key_pos = base_pos + begin_row - window + key_offsets
        logits = jnp.einsum("qhd,khd->hqk", q_rows, k_rows, preferred_element_type=f32) / math.sqrt(
            head_size
        )
        offset_bias = pos_table[:, None, :] + time_table[:, id_rows]
        scores = logits + skew_band(offset_bias)
        gap = query_pos[:, None] - key_pos[None, :]
        allowed = (
            (gap >= 0)
            & (gap < window)
            & (query_pos < length)[:, None]
            & (key_pos < length)[None, :]
            & (key_pos >= 0)[None, :]
        )
        weights = jnp.where(allowed, jax.nn.silu(scores) / window, 0.0).astype(jnp.bfloat16)
        return (begin_row, scores, allowed, weights, q_rows, k_rows, v_rows)

    def fwd_block(state, block_index):
        begin_row, scores, allowed, weights, q_rows, k_rows, v_rows = block_setup(block_index)
        mixed = jnp.einsum("hqk,khd->qhd", weights, v_rows, preferred_element_type=f32)
        return (state, mixed.reshape(window, width))

    _, mixed_blocks = lax.scan(fwd_block, jnp.zeros((), f32), jnp.arange(blocks, dtype=jnp.int32))
    attended = mixed_blocks.reshape(rows, width)
    att_hat, att_inv = norm_rows(attended)
    gated = (att_hat * gate_u.astype(f32)).astype(jnp.bfloat16)
    layer_out = (ev_float + jnp.dot(gated, w_out, preferred_element_type=f32)).astype(jnp.bfloat16)
    upstream = jnp.einsum("te,de->td", user_cot, w_out, preferred_element_type=f32)
    part_out = jnp.einsum("td,te->de", gated, user_cot, preferred_element_type=f32) * loss_scale
    grad_gate = upstream * att_hat
    grad_att = norm_back(upstream * gate_u.astype(f32), att_hat, att_inv).astype(jnp.bfloat16)

    def bwd_block(state, block_index):
        grad_keys, grad_values = state
        begin_row, scores, allowed, weights, q_rows, k_rows, v_rows = block_setup(block_index)
        grad_rows = lax.dynamic_slice_in_dim(grad_att, begin_row, window, 0).reshape(
            window, heads, head_size
        )
        grad_weights = jnp.einsum("qhd,khd->hqk", grad_rows, v_rows, preferred_element_type=f32)
        grad_v = jnp.einsum("hqk,qhd->khd", weights, grad_rows, preferred_element_type=f32).reshape(
            2 * window, width
        )
        grad_scores = jnp.where(allowed, grad_weights * silu_slope(scores) / window, 0.0).astype(
            jnp.bfloat16
        )
        grad_q = jnp.einsum(
            "hqk,khd->qhd", grad_scores, k_rows, preferred_element_type=f32
        ) / math.sqrt(head_size)
        grad_k = (
            jnp.einsum("hqk,qhd->khd", grad_scores, q_rows, preferred_element_type=f32)
            / math.sqrt(head_size)
        ).reshape(2 * window, width)
        grad_keys = lax.dynamic_update_slice_in_dim(
            grad_keys,
            lax.dynamic_slice_in_dim(grad_keys, begin_row, 2 * window, 0) + grad_k,
            begin_row,
            0,
        )
        grad_values = lax.dynamic_update_slice_in_dim(
            grad_values,
            lax.dynamic_slice_in_dim(grad_values, begin_row, 2 * window, 0) + grad_v,
            begin_row,
            0,
        )
        return ((grad_keys, grad_values), grad_q.reshape(window, width))

    empty = jnp.zeros((rows + window, width), f32)
    (grad_keys, grad_values), grad_q_blocks = lax.scan(
        bwd_block, (empty, empty), jnp.arange(blocks, dtype=jnp.int32)
    )
    back_keys, back_values = from_behind((grad_keys[:window], grad_values[:window]), "seq", -1)
    own_keys = jnp.concatenate([grad_keys[window:rows], grad_keys[rows:] + back_keys], axis=0)
    own_values = jnp.concatenate(
        [grad_values[window:rows], grad_values[rows:] + back_values], axis=0
    )
    grad_pre = (
        jnp.concatenate(
            [grad_gate, own_values, grad_q_blocks.reshape(rows, width), own_keys], axis=1
        )
        * silu_slope(pre_act)
    ).astype(jnp.bfloat16)
    part_in = jnp.einsum("td,tf->df", ev_normed, grad_pre, preferred_element_type=f32) * loss_scale
    part_bias = jnp.sum(grad_pre.astype(f32), axis=0) * loss_scale
    grad_normed = jnp.einsum("tf,df->td", grad_pre, w_in, preferred_element_type=f32)
    grad_events = (user_cot.astype(f32) + norm_back(grad_normed, ev_hat, ev_inv)).astype(
        jnp.bfloat16
    )
    sum_in, sum_bias, sum_out = lax.psum((part_in, part_bias, part_out), ("batch", "seq"))
    return (layer_out[None], grad_events[None], sum_in, sum_bias, sum_out)


def solution(mesh):
    placed = (
        P("batch", "seq", None),
        P("batch", "seq", None),
        P("batch", "seq", None),
        P("batch"),
        P(),
        P(),
        P(),
        P(),
        P(),
    )
    return jax.shard_map(
        on_device,
        mesh=mesh,
        in_specs=placed,
        out_specs=(P("batch", "seq", None), P("batch", "seq", None), P(), P(), P()),
        check_vma=False,
    )
```

profile of v0, /device:TPU:1, one launch (start us, length us, event | category | flops | bytes accessed | tf_op | source)
XLA Modules:
  0.0 897.9 jit_solution(17052017238184401304)
XLA Ops:
  7.2 1.1 convert_reduce_fusion.1
  8.3 1.1 fusion.57
  9.4 2.3 multiply_convert_fusion
  11.7 4.5 collective-permute-start.1
  16.2 1.9 collective-permute-start
  18.2 0.8 copy.42
  19.0 0.8 copy.44
  19.8 0.9 collective-permute-done.1
  20.8 1.1 collective-permute-done
  22.2 132.4 %while.30 = (s32[]{:T(128)}, f32[2,128,256]{1,2,0:T(8,128)S(1)}, s32[2]{0:T(128)S(1)}, bf16[384,256]{0,1:T(8,128)(2,1)S(1)}, s32[]{:T(128)}, /*index=5*/s32[]{:T...) while((s32[]{:T(128)}, f32[2,128,256]{1,2,0:T(8,128)S(1)}, ...), condition=%wide.region_3.4_spmd.clone, body=%wide.region_2.3_spmd.clone.sunk | while | flops 35359112 | bytes 7161440 | solution.py:118
  22.2 0.6 dynamic_slice.118
  23.4 0.7 fusion.122
  24.1 0.7 broadcast_compare_fusion.4
  24.9 0.9 fusion.121
  25.8 54.4 %gather_fusion = f32[16384,4]{1,0:T(8,128)} fusion(f32[4,128]{0,1:T(8,128)S(1)} %get-tuple-element.770, s32[16384]{0:T(1024)S(1)} %fusion.121), kind=kCustom, calls=%fused_computation.clone.clone.1 | custom fusion | bytes 589824 | tf_op jit(solution)/shard_map/while/body/eval_jaxpr/gather | solution.py:100
  80.2 5.2 copy.100
  86.1 0.7 reshape.259
  86.9 0.9 constant_dynamic-slice_fusion.18
  88.4 0.6 dynamic_slice.118
  89.6 0.7 fusion.122
  90.3 0.7 broadcast_compare_fusion.4
  91.1 0.9 fusion.121
  91.9 54.4 %gather_fusion = f32[16384,4]{1,0:T(8,128)} fusion(f32[4,128]{0,1:T(8,128)S(1)} %get-tuple-element.770, s32[16384]{0:T(1024)S(1)} %fusion.121), kind=kCustom, calls=%fused_computation.clone.clone.1 | custom fusion | bytes 589824 | tf_op jit(solution)/shard_map/while/body/eval_jaxpr/gather | solution.py:100
  146.4 5.2 copy.100
  152.3 0.7 reshape.259
  153.1 0.9 constant_dynamic-slice_fusion.18
  154.8 1.2 fusion.65
  156.1 1.0 multiply_convert_fusion.1
  157.1 141.9 %while.31 = (s32[]{:T(128)}, f32[384,256]{1,0:T(8,128)S(1)}, f32[384,256]{1,0:T(8,128)S(1)}, f32[2,128,256]{2,1,0:T(8,128)}, s32[2]{0:T(128)S(1)}, /*index=5*/bf...) while((s32[]{:T(128)}, f32[384,256]{1,0:T(8,128)S(1)}, ...), condition=%wide.region_9.10_spmd.clone, body=%wide.region_8.9_spmd.clone.sunk | while | flops 87362184 | bytes 17090756 | solution.py:163
  157.1 0.6 dynamic_slice.126
  158.4 0.9 fusion.134
  159.3 54.4 %gather_fusion.1 = f32[16384,4]{1,0:T(8,128)} fusion(f32[4,128]{0,1:T(8,128)S(1)} %get-tuple-element.836, s32[16384]{0:T(1024)S(1)} %fusion.134), kind=kCustom, calls=%fused_computation.1.clone.clone.1 | custom fusion | bytes 589824 | tf_op jit(solution)/shard_map/while/body/eval_jaxpr/gather | solution.py:100
  213.7 5.2 copy.104
  219.6 0.7 reshape.262
  220.4 0.9 constant_dynamic-slice_fusion.21
  221.6 0.7 fusion.137
  222.3 0.7 broadcast_compare_fusion.5
  223.1 0.9 constant_dynamic-slice_fusion.20
  224.1 0.6 copy-done.2
  225.6 1.1 fusion.139
  227.4 0.7 constant_dynamic-update-slice_fusion.9
  228.1 0.6 dynamic_slice.126
  229.4 0.9 fusion.134
  230.2 54.4 %gather_fusion.1 = f32[16384,4]{1,0:T(8,128)} fusion(f32[4,128]{0,1:T(8,128)S(1)} %get-tuple-element.836, s32[16384]{0:T(1024)S(1)} %fusion.134), kind=kCustom, calls=%fused_computation.1.clone.clone.1 | custom fusion | bytes 589824 | tf_op jit(solution)/shard_map/while/body/eval_jaxpr/gather | solution.py:100
  284.7 5.2 copy.104
  290.6 0.7 reshape.262
  291.4 0.9 constant_dynamic-slice_fusion.21
  292.5 0.7 fusion.137
  293.2 0.7 broadcast_compare_fusion.5
  294.0 0.9 constant_dynamic-slice_fusion.20
  295.0 0.6 copy-done.2
  296.5 1.1 fusion.139
  298.4 0.7 constant_dynamic-update-slice_fusion.9
  299.1 3.1 collective-permute-start.2
  302.2 1.9 collective-permute-start.3
  304.2 1.9 convolution_multiply_fusion.6
  306.1 1.9 fusion.44
  308.6 1.8 convert_reduce_fusion
  310.3 2.3 convolution_multiply_fusion.5
  313.4 110.6 %psum.22 = f32[1024]{0:T(1024)} all-reduce(f32[1024]{0:T(1024)S(1)} %broadcast_multiply_fusion), channel_id=1, replica_groups=mesh['batch'=32,'seq'=16] {'batch','seq'}, use_global_device_ids=true, to_apply=%region_14.15 | all-reduce | flops 1024 | bytes 8192 | tf_op jit(solution)/shard_map/psum | solution.py:183
  424.0 0.9 fusion.61
  424.8 462.3 %all-reduce.3.cloned.1.call-done = (f32[256,1024]{1,0:T(8,128)}, f32[256,256]{1,0:T(8,128)}) async-done(((f32[256,1024]{1,0:T(8,128)}, f32[256,256]{1,0:T(8,128)}), (f32[256,1024]{1,0:T(8,128)}, f32[256,256]{1,0:T(8,128)})) %all-reduce.3.cloned.1.call-update) | async-done | bytes 1310736 | tf_op jit(solution)/shard_map/psum | solution.py:183
  887.1 2.3 copy.136
  889.4 1.7 copy.137
  (132 shorter events, 10.6 us)
Async XLA Ops:
  7.2 2.2 copy-start
  7.2 15.0 %copy-start.6 = (f32[4,128]{1,0:T(4,128)S(1)}, f32[4,128]{1,0:T(4,128)}, u32[]{:S(2)}) copy-start(f32[4,128]{1,0:T(4,128)} %param.20) | copy-start | bytes 6148
  7.2 879.9 %all-reduce.3.cloned.1.call-start = ((), (), s32[]{:S(2)}) async-start(), calls=%async_computation | async-start | bytes 2621440 | tf_op jit(solution)/shard_map/psum | solution.py:183
  11.7 8.9 collective-permute-start.1
  16.2 5.7 collective-permute-start
  22.1 132.7 %copy-start.3 = (bf16[1,256,256]{2,1,0:T(8,128)(2,1)S(1)}, bf16[1,256,256]{2,1,0:T(8,128)(2,1)}, u32[]{:S(2)}) copy-start(bf16[1,256,256]{2,1,0:T(8,128)(2,1)} %param.14) | copy-start | bytes 393220
  223.0 1.0 copy-start.5
  224.0 0.6 copy-start.2
  294.0 1.0 copy-start.5
  295.0 0.6 copy-start.2
  299.1 14.1 %copy-start.1 = (bf16[1,256,256]{2,1,0:T(8,128)(2,1)S(1)}, bf16[1,256,256]{2,1,0:T(8,128)(2,1)}, u32[]{:S(2)}) copy-start(bf16[1,256,256]{2,1,0:T(8,128)(2,1)} %param.13) | copy-start | bytes 393220
  299.1 124.9 %copy-start.4 = (bf16[1,256,256]{2,1,0:T(8,128)(2,1)S(1)}, bf16[1,256,256]{2,1,0:T(8,128)(2,1)}, u32[]{:S(2)}) copy-start(bf16[1,256,256]{2,1,0:T(8,128)(2,1)} %param.14) | copy-start | bytes 393220
  299.1 8.9 collective-permute-start.2
  302.2 6.3 collective-permute-start.3
Sparse Core Ops, SparseCore 0:
  424.1 463.0 all-reduce.2
where the time goes:
time: 899 us; the launch traced here: 898 us
  waiting for transfers between devices  465 us (52%)
  local copies, waits for them, and re-layouts  261 us (29%)
  blocking collectives  111 us (12%)
  other arithmetic  16.4 us (2%)
  matrix products  15.4 us (2%)
  between operations  14.3 us (2%)
  starting transfers between devices  11.5 us (1%)
    psum x1, waiting for transfers between devices, on_device(): lax.psum((part_in, part_bias, part_out), ('batch', 'seq'))  462 us
    gather x8, local copies, waits for them, and re-layouts, block_setup(): offset_bias = pos_table[:, None, :] + time_table[:, id_rows]  239 us
    psum x1, blocking collectives, on_device(): lax.psum((part_in, part_bias, part_out), ('batch', 'seq'))  111 us
  transfers between devices with their start and end apart: 5, of which 4 were waited for; matrix products, arithmetic and copies ran while one was open for 1% of the time, Pallas kernels for 0%

commit v1 on v0

v1 whole, which is shorter than its diff:
```python
import functools
import math

import jax
import jax.numpy as jnp
from jax import lax
from jax.experimental import pallas as pl
from jax.experimental.pallas import tpu as pltpu
from jax.sharding import Mesh, PartitionSpec as P

EPS = 1e-05
F32 = jnp.float32
BF16 = jnp.bfloat16
NEAR = ("yl", "yh", "x", "c", "zl")
FAR = ("zh",)
BATCH = ("yl", "zh", "zl")
SEQ = ("yh", "x", "c")
TILE = 16
PIECE = 3 * TILE


def norm_rows(values):
    row_mean = jnp.mean(values, axis=-1, keepdims=True)
    centred = values - row_mean
    variance = jnp.mean(centred * centred, axis=-1, keepdims=True)
    inv_std = lax.rsqrt(variance + EPS)
    return (centred * inv_std, inv_std)


def norm_back(upstream, normed, inv_std):
    first = jnp.mean(upstream, axis=-1, keepdims=True)
    second = jnp.mean(upstream * normed, axis=-1, keepdims=True)
    return inv_std * (upstream - first - normed * second)


def silu_and_slope(pre_act):
    sigmoid = jax.nn.sigmoid(pre_act)
    value = pre_act * sigmoid
    return (value, sigmoid * (1.0 + pre_act * (1.0 - sigmoid)))


def dot(left, right, dims=((1,), (0,))):
    return lax.dot_general(left, right, (dims, ((), ())), preferred_element_type=F32)


ROWS_BY_ROWS = ((1,), (1,))
COLS_BY_COLS = ((0,), (0,))


def lane_gather(table, index):
    return jnp.take_along_axis(table, index, axis=1, mode="promise_in_bounds")


def layer_kernel(
    scale, length_ref, ev_ref, tail_ref, cot_ref, ids_ref, w_in_ref, b_in_ref, w_out_ref,
    pos_ref, time_ref, out_ref, parts_ref, own_ref, back_ref,
):
    rows, width = ev_ref.shape
    heads, window = pos_ref.shape
    head = width // heads
    slab = lax.axis_index(SEQ)
    real = length_ref[0] - slab * rows

    own_hat, _ = norm_rows(ev_ref[...].astype(F32))
    own_normed = own_hat.astype(BF16)
    tail_hat, _ = norm_rows(tail_ref[...].astype(F32))
    tail_normed = tail_hat.astype(BF16)

    def project(normed, first, last):
        columns = slice(first * width, last * width)
        pre_act = dot(normed, w_in_ref[:, columns]) + b_in_ref[:, columns]
        value, slope = silu_and_slope(pre_act)
        return (value.astype(BF16), slope)

    gate, gate_slope = project(own_normed, 0, 1)
    values, values_slope = project(own_normed, 1, 2)
    queries, queries_slope = project(own_normed, 2, 3)
    keys, keys_slope = project(own_normed, 3, 4)
    tail_values, tail_values_slope = project(tail_normed, 1, 2)
    tail_keys, tail_keys_slope = project(tail_normed, 3, 4)

    row = lax.broadcasted_iota(jnp.int32, (window, window), 0)
    lane = lax.broadcasted_iota(jnp.int32, (window, window), 1)
    offset = (row - lane) & (window - 1)
    stacked_row = jnp.concatenate([row] * heads, axis=0)
    stacked_lane = jnp.concatenate([lane] * heads, axis=0)
    recent = stacked_lane <= stacked_row
    pos_bias = [
        lane_gather(jnp.broadcast_to(pos_ref[h : h + 1, :], (window, window)), offset)
        for h in range(heads)
    ]
    times = [jnp.broadcast_to(time_ref[h : h + 1, :], (window, window)) for h in range(heads)]
    column_head = lax.broadcasted_iota(jnp.int32, (window, width), 1) // head

    def by_head(block):
        zero = jnp.zeros_like(block)
        return jnp.concatenate(
            [jnp.where(column_head == h, block, zero) for h in range(heads)], axis=0
        )

    def pick_heads(stack):
        total = stack[:window]
        for h in range(1, heads):
            total = jnp.where(column_head == h, stack[h * window : (h + 1) * window], total)
        return total

    def split_band(band):
        zero = jnp.zeros_like(band)
        return jnp.concatenate(
            [jnp.where(recent, band, zero), jnp.where(recent, zero, band)], axis=1
        ).astype(BF16)

    def join_band(pair):
        return jnp.where(recent, pair[:, :window], pair[:, window:])

    grad_gate, grad_queries, gated_blocks = [], [], []
    grad_keys, grad_values = [], []
    for block in range(rows // window):
        here = slice(block * window, (block + 1) * window)
        if block == 0:
            behind_keys, behind_values = tail_keys, tail_values
            behind_ok = slab > 0
        else:
            before = slice((block - 1) * window, block * window)
            behind_keys, behind_values = keys[before], values[before]
            behind_ok = True
        pair_keys = jnp.concatenate([keys[here], behind_keys], axis=0)
        pair_values = jnp.concatenate([values[here], behind_values], axis=0)
        stack_queries = by_head(queries[here])
        logits = join_band(dot(stack_queries, pair_keys, ROWS_BY_ROWS)) / math.sqrt(head)
        buckets = lane_gather(ids_ref[here, :], offset)
        bias = jnp.concatenate(
            [pos_bias[h] + lane_gather(times[h], buckets) for h in range(heads)], axis=0
        )
        scores = logits + bias
        allowed = stacked_row < real - block * window
        if block == 0:
            allowed = allowed & (recent | behind_ok)
        act, slope = silu_and_slope(scores)
        weights = split_band(jnp.where(allowed, act * (1.0 / window), 0.0))
        attended = pick_heads(dot(weights, pair_values))
        att_hat, att_inv = norm_rows(attended)
        gate_u = gate[here].astype(F32)
        gated = (att_hat * gate_u).astype(BF16)
        gated_blocks.append(gated)
        out_ref[here, :] = (ev_ref[here, :].astype(F32) + dot(gated, w_out_ref[...])).astype(BF16)
        upstream = dot(cot_ref[here, :], w_out_ref[...], ROWS_BY_ROWS)
        grad_gate.append(upstream * att_hat)
        grad_att = by_head(norm_back(upstream * gate_u, att_hat, att_inv).astype(BF16))
        grad_weights = join_band(dot(grad_att, pair_values, ROWS_BY_ROWS))
        grad_scores = split_band(jnp.where(allowed, grad_weights * slope * (1.0 / window), 0.0))
        pair_grad_values = dot(weights, grad_att, COLS_BY_COLS)
        pair_grad_keys = dot(grad_scores, stack_queries, COLS_BY_COLS) / math.sqrt(head)
        grad_queries.append(pick_heads(dot(grad_scores, pair_keys)) / math.sqrt(head))
        if block == 0:
            tail_grad_values = pair_grad_values[window:]
            tail_grad_keys = pair_grad_keys[window:]
        else:
            grad_values[-1] = grad_values[-1] + pair_grad_values[window:]
            grad_keys[-1] = grad_keys[-1] + pair_grad_keys[window:]
        grad_values.append(pair_grad_values[:window])
        grad_keys.append(pair_grad_keys[:window])

    def stacked(blocks):
        return jnp.concatenate(blocks, axis=0)

    own_pre = [
        (stacked(grad_gate) * gate_slope).astype(BF16),
        (stacked(grad_values) * values_slope).astype(BF16),
        (stacked(grad_queries) * queries_slope).astype(BF16),
        (stacked(grad_keys) * keys_slope).astype(BF16),
    ]
    tail_pre = {
        1: (tail_grad_values * tail_values_slope).astype(BF16),
        3: (tail_grad_keys * tail_keys_slope).astype(BF16),
    }
    own_total = None
    back_total = None
    bias_rows = []
    in_blocks = []
    for quarter in range(4):
        columns = slice(quarter * width, (quarter + 1) * width)
        part_in = dot(own_normed, own_pre[quarter], COLS_BY_COLS)
        part_bias = jnp.sum(own_pre[quarter].astype(F32), axis=0, keepdims=True)
        part = dot(own_pre[quarter], w_in_ref[:, columns], ROWS_BY_ROWS)
        own_total = part if own_total is None else own_total + part
        if quarter in tail_pre:
            part_in = part_in + dot(tail_normed, tail_pre[quarter], COLS_BY_COLS)
            part_bias = part_bias + jnp.sum(
                tail_pre[quarter].astype(F32), axis=0, keepdims=True
            )
            part = dot(tail_pre[quarter], w_in_ref[:, columns], ROWS_BY_ROWS)
            back_total = part if back_total is None else back_total + part
        in_blocks.append((part_in * scale).astype(BF16))
        bias_rows.append(part_bias * scale)
    own_ref[...] = own_total
    back_ref[...] = back_total
    part_out = dot(stacked(gated_blocks), cot_ref[...], COLS_BY_COLS) * scale

    low = lax.broadcasted_iota(jnp.int32, (TILE, 2 * 64), 1) < 64
    for quarter in range(4):
        half = part_out[:, (quarter // 2) * 128 : (quarter // 2 + 1) * 128]
        if quarter % 2:
            half = pltpu.roll(half, 64, 1)
        for group in range(16):
            piece = group * 4 + quarter
            here = slice(group * TILE, (group + 1) * TILE)
            for k in range(2):
                parts_ref[piece, k * TILE : (k + 1) * TILE, :] = in_blocks[quarter][
                    here, k * 128 : (k + 1) * 128
                ]
            if piece < 16:
                chunk = bias_rows[piece // 4][:, (piece // 2 % 2) * 128 : (piece // 2 % 2 + 1) * 128]
                if piece % 2 == 0:
                    chunk = pltpu.roll(chunk, 64, 1)
                chunk = jnp.broadcast_to(chunk, (TILE, 128))
            else:
                chunk = jnp.zeros((TILE, 128), F32)
            parts_ref[piece, 2 * TILE :, :] = jnp.where(low, half[here], chunk).astype(BF16)


def near_kernel(parts_ref, own_ref, back_ref, ev_ref, cot_ref, sum_ref, grad_ref):
    total = parts_ref[0].astype(F32)
    for i in range(1, parts_ref.shape[0]):
        total = total + parts_ref[i].astype(F32)
    for i in range(sum_ref.shape[0]):
        sum_ref[i] = total
    rows = ev_ref.shape[0]
    window = back_ref.shape[0]
    hat, inv = norm_rows(ev_ref[...].astype(F32))
    grad = jnp.concatenate(
        [own_ref[: rows - window, :], own_ref[rows - window :, :] + back_ref[...]], axis=0
    )
    grad_ref[...] = (cot_ref[...].astype(F32) + norm_back(grad, hat, inv)).astype(BF16)


def far_kernel(parts_ref, sum_ref):
    total = parts_ref[0]
    for i in range(1, parts_ref.shape[0]):
        total = total + parts_ref[i]
    total = total.astype(BF16)
    for i in range(sum_ref.shape[0]):
        sum_ref[i] = total


def unpack_kernel(all_ref, w_in_ref, b_in_ref, w_out_ref):
    for group in range(16):
        here = slice(group * TILE, (group + 1) * TILE)
        tiles = []
        for quarter in range(4):
            piece = group * 4 + quarter
            for k in range(2):
                first = quarter * 256 + k * 128
                w_in_ref[here, first : first + 128] = all_ref[
                    piece, k * TILE : (k + 1) * TILE, :
                ].astype(F32)
            tiles.append(all_ref[piece, 2 * TILE :, :].astype(F32))
        low = lax.broadcasted_iota(jnp.int32, (TILE, 128), 1) < 64
        for k in range(2):
            w_out_ref[here, k * 128 : (k + 1) * 128] = jnp.where(
                low, tiles[2 * k], pltpu.roll(tiles[2 * k + 1], 64, 1)
            )
        if group < 4:
            for k in range(2):
                b_in_ref[group * 2 + k : group * 2 + k + 1, :] = jnp.where(
                    low, pltpu.roll(tiles[2 * k], 64, 1), tiles[2 * k + 1]
                )[:1, :]


def call(kernel, outs, *args, scalars=0):
    return pl.pallas_call(
        kernel,
        out_shape=[jax.ShapeDtypeStruct(shape, kind) for shape, kind in outs],
        in_specs=[
            pl.BlockSpec(memory_space=pltpu.SMEM if i < scalars else pltpu.VMEM)
            for i in range(len(args))
        ],
        out_specs=[pl.BlockSpec(memory_space=pltpu.VMEM)] * len(outs),
        compiler_params=pltpu.CompilerParams(vmem_limit_bytes=48 * 1024 * 1024),
    )(*args)


def on_device(
    events, cotangent, bucket_ids, history_lengths, w_in, b_in, w_out, pos_table, time_table
):
    rows, width = events.shape[1:]
    window = pos_table.shape[1]
    slabs = lax.axis_size(SEQ)
    scale = 1.0 / math.sqrt(lax.axis_size(BATCH) * slabs * rows)
    own_events, own_cot = events[0], cotangent[0]
    near, far = lax.axis_size(NEAR), lax.axis_size(FAR)
    tail = lax.ppermute(
        own_events[rows - window :], SEQ, [(i, i + 1) for i in range(slabs - 1)]
    )
    layer_out, parts, own_grad, back_grad = call(
        functools.partial(layer_kernel, scale),
        [
            ((rows, width), BF16),
            ((near, PIECE, 128), BF16),
            ((rows, width), F32),
            ((window, width), F32),
        ],
        history_lengths, own_events, tail, own_cot, bucket_ids[0], w_in, b_in[None], w_out,
        pos_table, time_table,
        scalars=1,
    )
    back = lax.ppermute(back_grad, SEQ, [(i, i - 1) for i in range(1, slabs)])
    parts = lax.all_to_all(parts, NEAR, 0, 0)
    far_parts, grad_events = call(
        near_kernel,
        [((far, PIECE, 128), F32), ((rows, width), BF16)],
        parts, own_grad, back, own_events, own_cot,
    )
    far_parts = lax.all_to_all(far_parts, FAR, 0, 0)
    (sums,) = call(far_kernel, [((near, PIECE, 128), BF16)], far_parts)
    sums = lax.all_to_all(sums, NEAR, 0, 0)
    sum_in, sum_bias, sum_out = call(
        unpack_kernel, [((width, 4 * width), F32), ((8, 128), F32), ((width, width), F32)], sums
    )
    return (layer_out[None], grad_events[None], sum_in, sum_bias.reshape(4 * width), sum_out)


def solution(mesh):
    fine = Mesh(
        mesh.devices.reshape(2, 8, 2, 2, 4, 2), ("yl", "zh", "zl", "yh", "x", "c")
    )
    slabs = P(BATCH, SEQ, None)
    return jax.shard_map(
        on_device,
        mesh=fine,
        in_specs=(slabs, slabs, slabs, P(BATCH), P(), P(), P(), P(), P()),
        out_specs=(slabs, slabs, P(), P(), P()),
        check_vma=False,
    )
```

time: 899 us -> 96.6 us (0.11)
  waiting for transfers between devices: 465 us -> 15.9 us
  local copies, waits for them, and re-layouts: 261 us -> 5.35 us
  blocking collectives: 111 us -> 51.8 us
  other arithmetic: 16.4 us -> 0 us
  matrix products: 15.4 us -> 0 us
  between operations: 14.3 us -> 1.36 us
    psum x1 -> x0, waiting for transfers between devices: 462 us -> none  [on_device(): lax.psum((part_in, part_bias, part_out), ('batch', 'seq'))]
    gather x8 -> x0, local copies, waits for them, and re-layouts: 239 us -> none  [block_setup(): offset_bias = pos_table[:, None, :] + time_table[:, id_rows]]
    psum x1 -> x0, blocking collectives: 111 us -> none  [on_device(): lax.psum((part_in, part_bias, part_out), ('batch', 'seq'))]
    all_to_all x0 -> x2, blocking collectives: none -> 51.8 us  [the longest x1 32.9 us: on_device(): far_parts = lax.all_to_all(far_parts, FAR, 0, 0)]
    dot_general x18 -> x0, matrix products: 15.4 us -> none  [the longest x1 2.32 us: on_device(): jnp.einsum('td,tf->df', ev_normed, grad_pre, preferred_element_type=f32)]
    ppermute x4 -> x2, waiting for transfers between devices: 2.51 us -> 13.6 us  [the longest x1 9.93 us: on_device(): back = lax.ppermute(back_grad, SEQ, [(i, i - 1) for i in range(1, slabs)])]
  transfers between devices with their start and end apart: 5 -> 3, of which waited for: 4 -> 3; matrix products, arithmetic and copies ran while one was open for 1% -> 0% of each run, Pallas kernels for 0% -> 0%
where the time goes in v1:
time: 96.6 us; the launch traced here: 96.2 us
  blocking collectives  51.8 us (54%)
  waiting for transfers between devices  15.9 us (16%)
  starting transfers between devices  15.2 us (16%)
  Pallas kernels  6.56 us (7%)
  local copies, waits for them, and re-layouts  5.35 us (6%)
  between operations  1.36 us (1%)
    all_to_all x1, blocking collectives, on_device(): far_parts = lax.all_to_all(far_parts, FAR, 0, 0)  32.9 us
    all_to_all x1, blocking collectives, on_device(): sums = lax.all_to_all(sums, NEAR, 0, 0)  18.9 us
    ppermute x1, waiting for transfers between devices, on_device(): back = lax.ppermute(back_grad, SEQ, [(i, i - 1) for i in range(1, slabs)])  9.93 us
    all_to_all x1, starting transfers between devices, on_device(): parts = lax.all_to_all(parts, NEAR, 0, 0)  8.31 us
    pallas_call x4, Pallas kernels, call(): pl.pallas_call(kernel, out_shape=[jax.ShapeDtypeStruct(shape, kind) for s...  6.56 us
    ppermute x1, starting transfers between devices, on_device(): lax.ppermute(own_events[rows - window:], SEQ, [(i, i + 1) for i in range(...  4.5 us
    unnamed x18, local copies, waits for them, and re-layouts  4.44 us
    ppermute x1, waiting for transfers between devices, on_device(): lax.ppermute(own_events[rows - window:], SEQ, [(i, i + 1) for i in range(...  3.7 us
  transfers between devices with their start and end apart: 3, of which 3 were waited for; matrix products, arithmetic and copies ran while one was open for 0% of the time, Pallas kernels for 0%

profile of v1, /device:TPU:1, one launch (start us, length us, event | category | flops | bytes accessed | tf_op | source)
XLA Modules:
  0.0 96.2 jit_solution(14402502131048592638)
XLA Ops:
  0.6 0.0 copy-start
  0.6 0.9 slice_bitcast_fusion
  1.5 4.5 %collective-permute-start = (bf16[128,256]{1,0:T(8,128)(2,1)S(1)}, bf16[128,256]{1,0:T(8,128)(2,1)S(1)}, u32[]{:S(2)}, u32[]{:S(2)}) collective-permute-start(bf16[128,256]{1,0:T(8,128)(2,1)S(1)} %slice_bitcast_fusion), channel_id=1, source_target_pairs={{0,1},{1,2},{2,3},{3,4},{4,5},{5,6},{6,7},{7,8},{8,9},{9,10},{10,1... | collective-permute-start | bytes 196616 | tf_op jit(solution)/shard_map/ppermute | solution.py:292
  6.1 0.0 copy-start.8
  6.7 0.0 copy-start.6
  6.7 3.7 %collective-permute-done.tail_ref = bf16[128,256]{1,0:T(8,128)(2,1)S(1)} collective-permute-done((bf16[128,256]{1,0:T(8,128)(2,1)S(1)}, bf16[128,256]{1,0:T(8,128)(2,1)S(1)}, u32[]{:S(2)}, u32[]{:S(2)}) %collective-permute-start) | collective-permute-done | bytes 65568 | tf_op jit(solution)/shard_map/ppermute | solution.py:292
  10.4 0.0 copy-start.7
  10.4 0.0 copy-done
  10.4 0.0 copy-done.8
  10.4 0.0 copy-done.6
  10.5 0.7 copy-done.7
  11.1 0.0 copy-start.1
  11.1 1.0 %copy-done.1 = bf16[256,1024]{1,0:T(8,128)(2,1)S(1)} copy-done((bf16[256,1024]{1,0:T(8,128)(2,1)S(1)}, bf16[256,1024]{1,0:T(8,128)(2,1)}, u32[]{:S(2)}) %copy-start.1) | copy-done | bytes 524312
  12.2 0.0 copy-start.2
  12.2 0.9 copy-done.2
  13.1 0.0 copy-start.4
  13.1 0.9 copy-done.4
  14.0 0.0 copy-start.5
  14.0 0.9 copy-done.5
  14.9 4.4 %shard_map.128 = (bf16[256,256]{1,0:T(8,128)(2,1)}, bf16[64,48,128]{2,1,0:T(8,128)(2,1)}, f32[256,256]{1,0:T(8,128)S(1)}, f32[128,256]{1,0:T(8,128)S(1)}) custom-call(s32[1]{0:T(128)S(6)} %copy.14.length_ref, bf16[256,256]{1,0:T(8,128)(2,1)S(1)} %bitcast.9, bf16[128,256]{1,0:T(8,128)(2,1)S(1)} %collective-permute-done.tail_ref, ...), custom_call_target="tpu_custom_call" | custom-call | tf_op jit(solution)/shard_map/pallas_call | solution.py:271
  19.3 0.0 copy-start.3
  19.3 8.3 %all-to-all-start = ((bf16[64,48,128]{2,1,0:T(8,128)(2,1)}), bf16[64,48,128]{2,1,0:T(8,128)(2,1)S(1)}, u32[]{:S(2)}, u32[]{:S(2)}) async-start(bf16[64,48,128]{2,1,0:T(8,128)(2,1)} %get-tuple-element.15), calls=%async_computation | async-start | bytes 1572864 | tf_op jit(solution)/shard_map/all_to_all | solution.py:308
  27.6 2.4 %collective-permute-start.1 = (f32[128,256]{1,0:T(8,128)S(1)}, f32[128,256]{1,0:T(8,128)S(1)}, u32[]{:S(2)}, u32[]{:S(2)}) collective-permute-start(f32[128,256]{1,0:T(8,128)S(1)} %get-tuple-element.17), channel_id=1, source_target_pairs={{1,0},{2,1},{3,2},{4,3},{5,4},{6,5},{7,6},{8,7},{9,8},{10,9},{11,1... | collective-permute-start | bytes 393224 | tf_op jit(solution)/shard_map/ppermute | solution.py:307
  30.0 9.9 %collective-permute-done.1.back_ref = f32[128,256]{1,0:T(8,128)S(1)} collective-permute-done((f32[128,256]{1,0:T(8,128)S(1)}, f32[128,256]{1,0:T(8,128)S(1)}, u32[]{:S(2)}, u32[]{:S(2)}) %collective-permute-start.1) | collective-permute-done | bytes 131104 | tf_op jit(solution)/shard_map/ppermute | solution.py:307
  39.9 2.3 %all-to-all-done.parts_ref = bf16[64,48,128]{2,1,0:T(8,128)(2,1)S(1)} async-done(((bf16[64,48,128]{2,1,0:T(8,128)(2,1)}), bf16[64,48,128]{2,1,0:T(8,128)(2,1)S(1)}, u32[]{:S(2)}, u32[]{:S(2)}) %all-to-all-start) | async-done | bytes 786464 | tf_op jit(solution)/shard_map/all_to_all | solution.py:308
  42.2 0.0 copy-done.3
  42.2 1.0 shard_map.129
  43.1 32.9 %all_to_all.15.parts_ref = f32[8,48,128]{2,1,0:T(8,128)S(1)} all-to-all(f32[8,48,128]{2,1,0:T(8,128)S(1)} %get-tuple-element.19), channel_id=1, replica_groups=mesh['yl'=2,'zh'=8,'zl'=2,'yh'=2,'x'=4,'c'=2] {'zh'}, dimensions={0} | all-to-all | bytes 393216 | tf_op jit(solution)/shard_map/all_to_all | solution.py:314
  76.0 0.1 shard_map.130
  76.1 18.9 %all_to_all.16.all_ref = bf16[64,48,128]{2,1,0:T(8,128)(2,1)S(1)} all-to-all(bf16[64,48,128]{2,1,0:T(8,128)(2,1)S(1)} %shard_map.130), channel_id=1, replica_groups=mesh['yl'=2,'zh'=8,'zl'=2,'yh'=2,'x'=4,'c'=2] {'yl','yh','x','c','zl'}, dimensions={0} | all-to-all | bytes 1572864 | tf_op jit(solution)/shard_map/all_to_all | solution.py:316
  95.0 1.2 %shard_map.131 = (f32[256,1024]{1,0:T(8,128)}, f32[8,128]{1,0:T(8,128)}, f32[256,256]{1,0:T(8,128)}) custom-call(bf16[64,48,128]{2,1,0:T(8,128)(2,1)S(1)} %all_to_all.16.all_ref), custom_call_target="tpu_custom_call" | custom-call | tf_op jit(solution)/shard_map/pallas_call | solution.py:271
Async XLA Ops:
  0.6 9.8 %copy-start = (bf16[1,256,256]{2,1,0:T(8,128)(2,1)S(1)}, bf16[1,256,256]{2,1,0:T(8,128)(2,1)}, u32[]{:S(2)}) copy-start(bf16[1,256,256]{2,1,0:T(8,128)(2,1)} %param.9) | copy-start | bytes 393220
  1.5 8.9 %collective-permute-start = (bf16[128,256]{1,0:T(8,128)(2,1)S(1)}, bf16[128,256]{1,0:T(8,128)(2,1)S(1)}, u32[]{:S(2)}, u32[]{:S(2)}) collective-permute-start(bf16[128,256]{1,0:T(8,128)(2,1)S(1)} %slice_bitcast_fusion), channel_id=1, source_target_pairs={{0,1},{1,2},{2,3},{3,4},{4,5},{5,6},{6,7},{7,8},{8,9},{9,10},{10,1... | collective-permute-start | bytes 196616 | tf_op jit(solution)/shard_map/ppermute | solution.py:292
  6.1 4.4 %copy-start.8 = (f32[4,128]{1,0:T(4,128)S(1)}, f32[4,128]{1,0:T(4,128)}, u32[]{:S(2)}) copy-start(f32[4,128]{1,0:T(4,128)} %time_ref.1) | copy-start | bytes 6148
  6.7 3.7 %copy-start.6 = (f32[1024]{0:T(1024)S(1)}, f32[1024]{0:T(1024)}, u32[]{:S(2)}) copy-start(f32[1024]{0:T(1024)} %param.14) | copy-start | bytes 12292
  10.4 0.7 copy-start.7
  11.1 1.0 %copy-start.1 = (bf16[256,1024]{1,0:T(8,128)(2,1)S(1)}, bf16[256,1024]{1,0:T(8,128)(2,1)}, u32[]{:S(2)}) copy-start(bf16[256,1024]{1,0:T(8,128)(2,1)} %w_in_ref.1) | copy-start | bytes 1572868
  12.2 0.9 copy-start.2
  13.1 0.9 copy-start.4
  14.0 0.9 copy-start.5
  19.3 22.9 %copy-start.3 = (bf16[1,256,256]{2,1,0:T(8,128)(2,1)S(1)}, bf16[1,256,256]{2,1,0:T(8,128)(2,1)}, u32[]{:S(2)}) copy-start(bf16[1,256,256]{2,1,0:T(8,128)(2,1)} %param.10) | copy-start | bytes 393220
  19.3 22.9 %all-to-all-start = ((bf16[64,48,128]{2,1,0:T(8,128)(2,1)}), bf16[64,48,128]{2,1,0:T(8,128)(2,1)S(1)}, u32[]{:S(2)}, u32[]{:S(2)}) async-start(bf16[64,48,128]{2,1,0:T(8,128)(2,1)} %get-tuple-element.15), calls=%async_computation | async-start | bytes 1572864 | tf_op jit(solution)/shard_map/all_to_all | solution.py:308
  27.6 12.3 %collective-permute-start.1 = (f32[128,256]{1,0:T(8,128)S(1)}, f32[128,256]{1,0:T(8,128)S(1)}, u32[]{:S(2)}, u32[]{:S(2)}) collective-permute-start(f32[128,256]{1,0:T(8,128)S(1)} %get-tuple-element.17), channel_id=1, source_target_pairs={{1,0},{2,1},{3,2},{4,3},{5,4},{6,5},{7,6},{8,7},{9,8},{10,9},{11,1... | collective-permute-start | bytes 393224 | tf_op jit(solution)/shard_map/ppermute | solution.py:307

commit v2 on v1

v2 whole, which is shorter than its diff:
```python
import functools
import math

import jax
import jax.numpy as jnp
from jax import lax
from jax.experimental import pallas as pl
from jax.experimental.pallas import tpu as pltpu
from jax.sharding import Mesh, PartitionSpec as P

EPS = 1e-05
F32 = jnp.float32
BF16 = jnp.bfloat16
NEAR = ("yl", "yh", "x", "c", "zl")
FAR = ("zh",)
BATCH = ("yl", "zh", "zl")
SEQ = ("yh", "x", "c")
GROUP = 8
PIECE = 5 * GROUP


def norm_rows(values):
    row_mean = jnp.mean(values, axis=-1, keepdims=True)
    centred = values - row_mean
    variance = jnp.mean(centred * centred, axis=-1, keepdims=True)
    inv_std = lax.rsqrt(variance + EPS)
    return (centred * inv_std, inv_std)


def norm_back(upstream, normed, inv_std):
    first = jnp.mean(upstream, axis=-1, keepdims=True)
    second = jnp.mean(upstream * normed, axis=-1, keepdims=True)
    return inv_std * (upstream - first - normed * second)


def silu_and_slope(pre_act):
    sigmoid = jax.nn.sigmoid(pre_act)
    value = pre_act * sigmoid
    return (value, sigmoid * (1.0 + pre_act * (1.0 - sigmoid)))


def dot(left, right, dims=((1,), (0,))):
    return lax.dot_general(left, right, (dims, ((), ())), preferred_element_type=F32)


ROWS_BY_ROWS = ((1,), (1,))
COLS_BY_COLS = ((0,), (0,))


def lane_gather(table, index):
    return jnp.take_along_axis(table, index, axis=1, mode="promise_in_bounds")


class Band:
    def __init__(self, heads, window, width):
        self.heads, self.window, self.head = heads, window, width // heads
        row = lax.broadcasted_iota(jnp.int32, (window, window), 0)
        lane = lax.broadcasted_iota(jnp.int32, (window, window), 1)
        self.offset = (row - lane) & (window - 1)
        self.row = jnp.concatenate([row] * heads, axis=0)
        self.recent = jnp.concatenate([lane <= row] * heads, axis=0)
        self.column_head = lax.broadcasted_iota(jnp.int32, (window, width), 1) // self.head

    def bias(self, bucket_rows, pos_ref, time_ref):
        shape = (self.window, self.window)
        buckets = lane_gather(bucket_rows, self.offset)
        return jnp.concatenate(
            [
                lane_gather(jnp.broadcast_to(pos_ref[h : h + 1, :], shape), self.offset)
                + lane_gather(jnp.broadcast_to(time_ref[h : h + 1, :], shape), buckets)
                for h in range(self.heads)
            ],
            axis=0,
        )

    def by_head(self, block):
        zero = jnp.zeros_like(block)
        return jnp.concatenate(
            [jnp.where(self.column_head == h, block, zero) for h in range(self.heads)], axis=0
        )

    def pick_heads(self, stack):
        total = stack[: self.window]
        for h in range(1, self.heads):
            part = stack[h * self.window : (h + 1) * self.window]
            total = jnp.where(self.column_head == h, part, total)
        return total

    def split(self, band):
        zero = jnp.zeros_like(band)
        return jnp.concatenate(
            [jnp.where(self.recent, band, zero), jnp.where(self.recent, zero, band)], axis=1
        ).astype(BF16)

    def join(self, pair):
        return jnp.where(self.recent, pair[:, : self.window], pair[:, self.window :])

    def block(self, queries, pair_keys, pair_values, gate, bias, allowed, ev, cot, w_out):
        root = math.sqrt(self.head)
        stack_queries = self.by_head(queries)
        scores = self.join(dot(stack_queries, pair_keys, ROWS_BY_ROWS)) / root + bias
        act, slope = silu_and_slope(scores)
        weights = self.split(jnp.where(allowed, act * (1.0 / self.window), 0.0))
        att_hat, att_inv = norm_rows(self.pick_heads(dot(weights, pair_values)))
        gate_u = gate.astype(F32)
        gated = (att_hat * gate_u).astype(BF16)
        out = (ev.astype(F32) + dot(gated, w_out)).astype(BF16)
        upstream = dot(cot, w_out, ROWS_BY_ROWS)
        grad_att = self.by_head(norm_back(upstream * gate_u, att_hat, att_inv).astype(BF16))
        grad_weights = self.join(dot(grad_att, pair_values, ROWS_BY_ROWS))
        grad_scores = self.split(
            jnp.where(allowed, grad_weights * slope * (1.0 / self.window), 0.0)
        )
        grad_values = dot(weights, grad_att, COLS_BY_COLS)
        grad_queries = self.pick_heads(dot(grad_scores, pair_keys)) / root
        grad_keys = dot(grad_scores, stack_queries, COLS_BY_COLS) / root
        return (out, gated, upstream * att_hat, grad_values, grad_queries, grad_keys)


def own_kernel(
    length_ref, ev_hbm, cot_hbm, ids_hbm, w_in_hbm, b_in_hbm, w_out_hbm, pos_hbm, time_hbm,
    out_ref, gated_ref, pre_ref, own_ref, normed_ref, proj_ref, slope_ref, bias_ref, grads_ref,
    ev_ref, cot_ref, w_in_ref, b_in_ref, w_out_ref,
    ids_ref, pos_ref, time_ref, sems,
):
    pairs = [
        (ev_hbm, ev_ref), (w_in_hbm, w_in_ref), (b_in_hbm, b_in_ref), (ids_hbm, ids_ref),
        (pos_hbm, pos_ref), (time_hbm, time_ref), (cot_hbm, cot_ref), (w_out_hbm, w_out_ref),
    ]
    copies = [pltpu.make_async_copy(a, b, sems.at[i]) for i, (a, b) in enumerate(pairs)]
    for copy in copies:
        copy.start()
    rows, width = ev_ref.shape
    heads, window = pos_ref.shape
    real = length_ref[0] - lax.axis_index(SEQ) * rows
    band = Band(heads, window, width)
    copies[0].wait()
    hat, _ = norm_rows(ev_ref[...].astype(F32))
    normed = hat.astype(BF16)
    normed_ref[...] = normed
    copies[1].wait()
    copies[2].wait()
    value, slope = silu_and_slope(dot(normed, w_in_ref[...]) + b_in_ref[...])
    projected = value.astype(BF16)
    first, last = slice(0, window), slice(window, 2 * window)
    proj_ref[...] = projected[first]
    slope_ref[...] = slope[first]
    gate, values, queries, keys = [projected[:, i * width : (i + 1) * width] for i in range(4)]
    for copy in copies[3:6]:
        copy.wait()
    bias_ref[...] = band.bias(ids_ref[first, :], pos_ref, time_ref)
    bias = band.bias(ids_ref[last, :], pos_ref, time_ref)
    copies[6].wait()
    copies[7].wait()
    out, gated, grad_gate, grad_values, grad_queries, grad_keys = band.block(
        queries[last],
        jnp.concatenate([keys[last], keys[first]], axis=0),
        jnp.concatenate([values[last], values[first]], axis=0),
        gate[last], bias, band.row < real - window, ev_ref[last, :], cot_ref[last, :],
        w_out_ref[...],
    )
    out_ref[...] = out
    gated_ref[...] = gated
    grads_ref[:, :width] = grad_values[window:]
    grads_ref[:, width:] = grad_keys[window:]
    grads = jnp.concatenate(
        [grad_gate, grad_values[:window], grad_queries, grad_keys[:window]], axis=1
    )
    pre = (grads * slope[last]).astype(BF16)
    pre_ref[...] = pre
    own_ref[...] = dot(pre, w_in_ref[...], ROWS_BY_ROWS)


def edge_kernel(
    scale, length_ref, moved_ref, out_last_ref, gated_ref, pre_ref, normed_ref, proj_ref,
    slope_ref, bias_ref, grads_ref, ev_ref, cot_ref, w_in_ref, b_in_ref, w_out_ref,
    out_ref, parts_ref, bias_out_ref, own_ref, back_ref,
):
    rows, width = ev_ref.shape
    window = out_last_ref.shape[0]
    heads = bias_ref.shape[0] // window
    slab = lax.axis_index(SEQ)
    real = length_ref[0] - slab * rows
    band = Band(heads, window, width)
    first, last = slice(0, window), slice(window, 2 * window)
    tail_hat, _ = norm_rows(moved_ref[0, rows - window :, :].astype(F32))
    tail_normed = tail_hat.astype(BF16)

    def columns(i):
        return slice(i * width, (i + 1) * width)

    def project(i):
        pre_act = dot(tail_normed, w_in_ref[:, columns(i)]) + b_in_ref[:, columns(i)]
        value, slope = silu_and_slope(pre_act)
        return (value.astype(BF16), slope)

    tail_values, tail_values_slope = project(1)
    tail_keys, tail_keys_slope = project(3)
    gate, values, queries, keys = [proj_ref[:, columns(i)] for i in range(4)]
    out, gated, grad_gate, grad_values, grad_queries, grad_keys = band.block(
        queries,
        jnp.concatenate([keys, tail_keys], axis=0),
        jnp.concatenate([values, tail_values], axis=0),
        gate, bias_ref[...], (band.row < real) & (band.recent | (slab > 0)),
        ev_ref[first, :], cot_ref[first, :], w_out_ref[...],
    )
    out_ref[first, :] = out
    out_ref[last, :] = out_last_ref[...]
    grads = [
        grad_gate,
        grad_values[:window] + grads_ref[:, :width],
        grad_queries,
        grad_keys[:window] + grads_ref[:, width:],
    ]
    tail_pre = {
        1: (grad_values[window:] * tail_values_slope).astype(BF16),
        3: (grad_keys[window:] * tail_keys_slope).astype(BF16),
    }
    left = jnp.concatenate([normed_ref[...], tail_normed], axis=0)
    own_total, back_total, in_blocks, bias_rows = None, None, [], []
    for i in range(4):
        own_pre = (grads[i] * slope_ref[:, columns(i)]).astype(BF16)
        part = dot(own_pre, w_in_ref[:, columns(i)], ROWS_BY_ROWS)
        own_total = part if own_total is None else own_total + part
        right = [own_pre, pre_ref[:, columns(i)]]
        if i in tail_pre:
            part = dot(tail_pre[i], w_in_ref[:, columns(i)], ROWS_BY_ROWS)
            back_total = part if back_total is None else back_total + part
            right.append(tail_pre[i])
        right = jnp.concatenate(right, axis=0)
        in_blocks.append(dot(left[: right.shape[0]], right, COLS_BY_COLS) * scale)
        bias_rows.append(jnp.sum(right.astype(F32), axis=0, keepdims=True) * scale)
    own_ref[...] = own_total
    back_ref[...] = back_total
    part_out = dot(
        jnp.concatenate([gated, gated_ref[...]], axis=0), cot_ref[...], COLS_BY_COLS
    ) * scale
    for i in range(8):
        bias_out_ref[i : i + 1, :] = bias_rows[i // 2][:, (i % 2) * 128 : (i % 2 + 1) * 128]
    for group in range(width // GROUP):
        here = slice(group * GROUP, (group + 1) * GROUP)
        for half in range(2):
            tiles = [
                in_blocks[2 * half + k // 2][here, (k % 2) * 128 : (k % 2 + 1) * 128]
                for k in range(4)
            ]
            tiles.append(part_out[here, half * 128 : (half + 1) * 128])
            parts_ref[2 * group + half] = jnp.concatenate(tiles, axis=0).astype(BF16)


def near_kernel(parts_ref, bias_ref, sum_ref):
    total = parts_ref[0].astype(F32)
    for i in range(1, parts_ref.shape[0]):
        total = total + parts_ref[i].astype(F32)
    sums = jnp.concatenate([total, bias_ref[...]], axis=0).astype(BF16)
    for i in range(sum_ref.shape[0]):
        sum_ref[i] = sums


def far_kernel(parts_ref, sum_ref):
    total = parts_ref[0].astype(F32)
    for i in range(1, parts_ref.shape[0]):
        total = total + parts_ref[i].astype(F32)
    sums = total.astype(BF16)
    for i in range(sum_ref.shape[0]):
        sum_ref[i] = sums


def unpack_kernel(all_ref, w_in_ref, b_in_ref, w_out_ref):
    bias = None
    for piece in range(all_ref.shape[0]):
        rows = all_ref[piece].astype(F32)
        group, half = piece // 2, piece % 2
        here = slice(group * GROUP, (group + 1) * GROUP)
        tiles = [rows[k * GROUP : (k + 1) * GROUP] for k in range(6)]
        w_in_ref[here, half * 512 : (half + 1) * 512] = jnp.concatenate(tiles[:4], axis=1)
        w_out_ref[here, half * 128 : (half + 1) * 128] = tiles[4]
        bias = tiles[5] if bias is None else bias + tiles[5]
    b_in_ref[...] = bias


def grad_kernel(own_first_ref, own_last_ref, back_ref, ev_ref, cot_ref, grad_ref):
    window = back_ref.shape[0]
    for half, grad in enumerate((own_first_ref[...], own_last_ref[...] + back_ref[...])):
        here = slice(half * window, (half + 1) * window)
        hat, inv = norm_rows(ev_ref[here, :].astype(F32))
        grad_ref[here, :] = (cot_ref[here, :].astype(F32) + norm_back(grad, hat, inv)).astype(BF16)


def call(kernel, outs, *args, spaces=None, scratch=(), flops=0, moved=0):
    spaces = spaces or [pltpu.VMEM] * len(args)
    args = [
        pltpu.with_memory_space_constraint(arg, space) if space == pltpu.HBM else arg
        for arg, space in zip(args, spaces)
    ]
    return pl.pallas_call(
        kernel,
        out_shape=[
            pltpu.VMEM(shape, kind) if kept else jax.ShapeDtypeStruct(shape, kind)
            for shape, kind, *kept in outs
        ],
        in_specs=[pl.BlockSpec(memory_space=space) for space in spaces],
        out_specs=[pl.BlockSpec(memory_space=pltpu.VMEM)] * len(outs),
        scratch_shapes=scratch,
        compiler_params=pltpu.CompilerParams(vmem_limit_bytes=24 * 1024 * 1024),
        cost_estimate=pl.CostEstimate(flops=flops, bytes_accessed=moved, transcendentals=0),
    )(*args)


def on_device(
    events, cotangent, bucket_ids, history_lengths, w_in, b_in, w_out, pos_table, time_table
):
    rows, width = events.shape[1:]
    heads, window = pos_table.shape
    slabs = lax.axis_size(SEQ)
    scale = 1.0 / math.sqrt(lax.axis_size(BATCH) * slabs * rows)
    near, far = lax.axis_size(NEAR), lax.axis_size(FAR)
    moved = lax.ppermute(events, SEQ, [(i, i + 1) for i in range(slabs - 1)])
    half = (window, width)
    (
        out_last, gated, pre, own_last, normed, proj, slope, bias, grads, ev, cot, w_in_near,
        b_in_near, w_out_near,
    ) = call(
        own_kernel,
        [
            (half, BF16), (half, BF16), ((window, 4 * width), BF16), (half, F32),
            ((rows, width), BF16), ((window, 4 * width), BF16), ((window, 4 * width), F32),
            ((heads * window, window), F32), ((window, 2 * width), F32), ((rows, width), BF16),
            ((rows, width), BF16), (w_in.shape, BF16), ((1, 4 * width), F32), (w_out.shape, BF16),
        ],
        history_lengths, events[0], cotangent[0], bucket_ids[0], w_in, b_in[None], w_out,
        pos_table, time_table,
        spaces=[pltpu.SMEM] + [pltpu.HBM] * 8,
        scratch=[
            pltpu.VMEM((rows, window), jnp.int32),
            pltpu.VMEM(pos_table.shape, F32),
            pltpu.VMEM(time_table.shape, F32),
            pltpu.SemaphoreType.DMA((8,)),
        ],
        flops=10**9, moved=10**7,
    )
    layer_out, parts, bias_part, own_first, back = call(
        functools.partial(edge_kernel, scale),
        [
            ((rows, width), BF16), ((near, PIECE, 128), BF16), ((8, 128), F32), (half, F32),
            (half, F32),
        ],
        history_lengths, moved, out_last, gated, pre, normed, proj, slope, bias, grads, ev, cot,
        w_in_near, b_in_near, w_out_near,
        spaces=[pltpu.SMEM] + [pltpu.VMEM] * 14,
        flops=10**9, moved=10**7,
    )
    back = lax.ppermute(back, SEQ, [(i, i - 1) for i in range(1, slabs)])
    parts = lax.all_to_all(parts, NEAR, 0, 0)
    (grad_events,) = call(
        grad_kernel, [((rows, width), BF16)], own_first, own_last, back, ev, cot,
        flops=10**7, moved=10**6,
    )
    (sums,) = call(near_kernel, [((far, PIECE + GROUP, 128), BF16)], parts, bias_part)
    sums = lax.all_to_all(sums, FAR, 0, 0)
    (sums,) = call(far_kernel, [((near, PIECE + GROUP, 128), BF16)], sums)
    sums = lax.all_to_all(sums, NEAR, 0, 0)
    sum_in, sum_bias, sum_out = call(
        unpack_kernel, [((width, 4 * width), F32), ((8, 128), F32), ((width, width), F32)], sums
    )
    return (layer_out[None], grad_events[None], sum_in, sum_bias.reshape(4 * width), sum_out)


def solution(mesh):
    fine = Mesh(
        mesh.devices.reshape(2, 8, 2, 2, 4, 2), ("yl", "zh", "zl", "yh", "x", "c")
    )
    slabs = P(BATCH, SEQ, None)
    return jax.shard_map(
        on_device,
        mesh=fine,
        in_specs=(slabs, slabs, slabs, P(BATCH), P(), P(), P(), P(), P()),
        out_specs=(slabs, slabs, P(), P(), P()),
        check_vma=False,
    )
```

time: 96.6 us -> 85 us (0.88)
  local copies, waits for them, and re-layouts: 5.35 us -> 0 us
  waiting for transfers between devices: 15.9 us -> 11.4 us
  Pallas kernels: 6.56 us -> 9.69 us
  blocking collectives: 51.8 us -> 48.7 us
  starting transfers between devices: 15.2 us -> 13.5 us
    unnamed x18 -> x0, local copies, waits for them, and re-layouts: 4.44 us -> none
    ppermute x2, waiting for transfers between devices: 13.6 us -> 10 us  [the longest x1 9.93 us: on_device(): back = lax.ppermute(back, SEQ, [(i, i - 1) for i in range(1, slabs)])]
    pallas_call x4 -> x6, Pallas kernels: 6.56 us -> 9.69 us  [call(): pl.pallas_call(kernel, out_shape=[pltpu.VMEM(shape, kind) if kept else ja...]
    all_to_all x2, blocking collectives: 51.8 us -> 48.7 us  [the longest x1 26.9 us: on_device(): sums = lax.all_to_all(sums, FAR, 0, 0)]
    all_to_all x1, starting transfers between devices: 8.31 us -> 6.67 us  [on_device(): sums = lax.all_to_all(sums, NEAR, 0, 0)]
  transfers between devices with their start and end apart: 3 -> 3, of which waited for: 3 -> 3; matrix products, arithmetic and copies ran while one was open for 0% -> 0% of each run, Pallas kernels for 0% -> 6%
where the time goes in v2:
time: 85 us; the launch traced here: 84.6 us
  blocking collectives  48.7 us (57%)
  starting transfers between devices  13.5 us (16%)
  waiting for transfers between devices  11.4 us (13%)
  Pallas kernels  9.69 us (11%)
  between operations  1.32 us (2%)
    all_to_all x1, blocking collectives, on_device(): sums = lax.all_to_all(sums, FAR, 0, 0)  26.9 us
    all_to_all x1, blocking collectives, on_device(): parts = lax.all_to_all(parts, NEAR, 0, 0)  21.9 us
    ppermute x1, waiting for transfers between devices, on_device(): back = lax.ppermute(back, SEQ, [(i, i - 1) for i in range(1, slabs)])  9.93 us
    pallas_call x6, Pallas kernels, call(): pl.pallas_call(kernel, out_shape=[pltpu.VMEM(shape, kind) if kept else ja...  9.69 us
    all_to_all x1, starting transfers between devices, on_device(): sums = lax.all_to_all(sums, NEAR, 0, 0)  6.67 us
    ppermute x1, starting transfers between devices, on_device(): moved = lax.ppermute(events, SEQ, [(i, i + 1) for i in range(slabs - 1)])  4.51 us
    ppermute x1, starting transfers between devices, on_device(): back = lax.ppermute(back, SEQ, [(i, i - 1) for i in range(1, slabs)])  2.36 us
  transfers between devices with their start and end apart: 3, of which 3 were waited for; matrix products, arithmetic and copies ran while one was open for 0% of the time, Pallas kernels for 6%

profile of v2, /device:TPU:1, one launch (start us, length us, event | category | flops | bytes accessed | tf_op | source)
XLA Modules:
  0.0 84.6 jit_solution(18021395081292868594)
XLA Ops:
  0.6 4.5 %collective-permute-start = (bf16[1,256,256]{2,1,0:T(8,128)(2,1)}, bf16[1,256,256]{2,1,0:T(8,128)(2,1)S(1)}, u32[]{:S(2)}, u32[]{:S(2)}) collective-permute-start(bf16[1,256,256]{2,1,0:T(8,128)(2,1)} %param.9), channel_id=1, source_target_pairs={{0,1},{1,2},{2,3},{3,4},{4,5},{5,6},{6,7},{7,8},{8,9},{9,10},{10,1... | collective-permute-start | bytes 393224 | tf_op jit(solution)/shard_map/ppermute | solution.py:318
  5.8 3.9 %shard_map.128 = (bf16[128,256]{1,0:T(8,128)(2,1)S(1)}, bf16[128,256]{1,0:T(8,128)(2,1)S(1)}, bf16[128,1024]{1,0:T(8,128)(2,1)S(1)}, f32[128,256]{1,0:T(8,128)S(...) custom-call(s32[1]{0:T(128)S(6)} %copy.14.length_ref, ...), custom_call_target="tpu_custom_call" | custom-call | flops 1000000000 | bytes 10000000 | tf_op jit(solution)/shard_map/pallas_call | solution.py:296
  9.7 0.1 collective-permute-done.moved_ref
  9.8 2.6 %shard_map.129 = (bf16[256,256]{1,0:T(8,128)(2,1)}, bf16[64,40,128]{2,1,0:T(8,128)(2,1)S(1)}, f32[8,128]{1,0:T(8,128)S(1)}, f32[128,256]{1,0:T(8,128)S(1)}, f32[128,256]{1,0:T(8,128)S(1)}) custom-call(s32[1]{0:T(128)S(6)} %copy.14.length_ref, bf16[1,256,256]{2,1,0:T(8,128)(2,1)S(1)} %collective-permute-done.moved_ref, ...), custom_call_target="tpu_custom_call" | custom-call | flops 1000000000 | bytes 10000000 | tf_op jit(solution)/shard_map/pallas_call | solution.py:296
  12.4 21.9 %all_to_all.15.parts_ref = bf16[64,40,128]{2,1,0:T(8,128)(2,1)S(1)} all-to-all(bf16[64,40,128]{2,1,0:T(8,128)(2,1)S(1)} %get-tuple-element.44), channel_id=1, replica_groups=mesh['yl'=2,'zh'=8,'zl'=2,'yh'=2,'x'=4,'c'=2] {'yl','yh','x','c','zl'}, dimensions={0} | all-to-all | bytes 1310720 | tf_op jit(solution)/shard_map/all_to_all | solution.py:354
  34.3 0.1 shard_map.131
  34.4 26.9 %all_to_all.16.parts_ref = bf16[8,48,128]{2,1,0:T(8,128)(2,1)S(1)} all-to-all(bf16[8,48,128]{2,1,0:T(8,128)(2,1)S(1)} %shard_map.131), channel_id=1, replica_groups=mesh['yl'=2,'zh'=8,'zl'=2,'yh'=2,'x'=4,'c'=2] {'zh'}, dimensions={0} | all-to-all | bytes 196608 | tf_op jit(solution)/shard_map/all_to_all | solution.py:360
  61.3 0.9 %shard_map.132 = bf16[64,48,128]{2,1,0:T(8,128)(2,1)} custom-call(bf16[8,48,128]{2,1,0:T(8,128)(2,1)S(1)} %all_to_all.16.parts_ref), custom_call_target="tpu_custom_call" | custom-call | tf_op jit(solution)/shard_map/pallas_call | solution.py:296
  62.2 6.7 %all-to-all-start.2 = ((bf16[64,48,128]{2,1,0:T(8,128)(2,1)}), bf16[64,48,128]{2,1,0:T(8,128)(2,1)S(1)}, u32[]{:S(2)}, u32[]{:S(2)}) async-start(bf16[64,48,128]{2,1,0:T(8,128)(2,1)} %shard_map.132), calls=%async_computation.2 | async-start | bytes 1572864 | tf_op jit(solution)/shard_map/all_to_all | solution.py:362
  68.9 2.4 %collective-permute-start.1 = (f32[128,256]{1,0:T(8,128)S(1)}, f32[128,256]{1,0:T(8,128)S(1)}, u32[]{:S(2)}, u32[]{:S(2)}) collective-permute-start(f32[128,256]{1,0:T(8,128)S(1)} %get-tuple-element.43), channel_id=1, source_target_pairs={{1,0},{2,1},{3,2},{4,3},{5,4},{6,5},{7,6},{8,7},{9,8},{10,9},{11,1... | collective-permute-start | bytes 393224 | tf_op jit(solution)/shard_map/ppermute | solution.py:353
  71.3 9.9 %collective-permute-done.1.back_ref = f32[128,256]{1,0:T(8,128)S(1)} collective-permute-done((f32[128,256]{1,0:T(8,128)S(1)}, f32[128,256]{1,0:T(8,128)S(1)}, u32[]{:S(2)}, u32[]{:S(2)}) %collective-permute-start.1) | collective-permute-done | bytes 131104 | tf_op jit(solution)/shard_map/ppermute | solution.py:353
  81.2 1.0 %shard_map.130 = bf16[256,256]{1,0:T(8,128)(2,1)} custom-call(f32[128,256]{1,0:T(8,128)S(1)} %get-tuple-element.41.own_first_ref, f32[128,256]{1,0:T(8,128)S(1)} %get-tuple-element.42.own_last_ref, f32[128,256]{1,0:T(8,128)S(1)} %collective-permute-done.1.back_ref, bf16[256,256]{1,0:T(8,128)(2,1)S(1)} %get-tuple-element.35.ev_ref, ...), custom_call_target="tpu_custom_call" | custom-call | flops 10000000 | bytes 1000000 | tf_op jit(solution)/shard_map/pallas_call | solution.py:296
  82.2 1.3 %all-to-all-done.2.all_ref = bf16[64,48,128]{2,1,0:T(8,128)(2,1)S(1)} async-done(((bf16[64,48,128]{2,1,0:T(8,128)(2,1)}), bf16[64,48,128]{2,1,0:T(8,128)(2,1)S(1)}, u32[]{:S(2)}, u32[]{:S(2)}) %all-to-all-start.2) | async-done | bytes 786464 | tf_op jit(solution)/shard_map/all_to_all | solution.py:362
  83.5 1.1 %shard_map.133 = (f32[256,1024]{1,0:T(8,128)}, f32[8,128]{1,0:T(8,128)}, f32[256,256]{1,0:T(8,128)}) custom-call(bf16[64,48,128]{2,1,0:T(8,128)(2,1)S(1)} %all-to-all-done.2.all_ref), custom_call_target="tpu_custom_call" | custom-call | tf_op jit(solution)/shard_map/pallas_call | solution.py:296
Async XLA Ops:
  0.6 9.2 %collective-permute-start = (bf16[1,256,256]{2,1,0:T(8,128)(2,1)}, bf16[1,256,256]{2,1,0:T(8,128)(2,1)S(1)}, u32[]{:S(2)}, u32[]{:S(2)}) collective-permute-start(bf16[1,256,256]{2,1,0:T(8,128)(2,1)} %param.9), channel_id=1, source_target_pairs={{0,1},{1,2},{2,3},{3,4},{4,5},{5,6},{6,7},{7,8},{8,9},{9,10},{10,1... | collective-permute-start | bytes 393224 | tf_op jit(solution)/shard_map/ppermute | solution.py:318
  62.2 21.3 %all-to-all-start.2 = ((bf16[64,48,128]{2,1,0:T(8,128)(2,1)}), bf16[64,48,128]{2,1,0:T(8,128)(2,1)S(1)}, u32[]{:S(2)}, u32[]{:S(2)}) async-start(bf16[64,48,128]{2,1,0:T(8,128)(2,1)} %shard_map.132), calls=%async_computation.2 | async-start | bytes 1572864 | tf_op jit(solution)/shard_map/all_to_all | solution.py:362
  68.9 12.3 %collective-permute-start.1 = (f32[128,256]{1,0:T(8,128)S(1)}, f32[128,256]{1,0:T(8,128)S(1)}, u32[]{:S(2)}, u32[]{:S(2)}) collective-permute-start(f32[128,256]{1,0:T(8,128)S(1)} %get-tuple-element.43), channel_id=1, source_target_pairs={{1,0},{2,1},{3,2},{4,3},{5,4},{6,5},{7,6},{8,7},{9,8},{10,9},{11,1... | collective-permute-start | bytes 393224 | tf_op jit(solution)/shard_map/ppermute | solution.py:353

commit v3 on v2

--- a/solution.py
+++ b/solution.py
@@ -17,6 +17,7 @@
 SEQ = ("yh", "x", "c")
 GROUP = 8
 PIECE = 5 * GROUP
+KEPT = True
 
 
 def norm_rows(values):
@@ -248,7 +249,8 @@
             parts_ref[2 * group + half] = jnp.concatenate(tiles, axis=0).astype(BF16)
 
 
-def near_kernel(parts_ref, bias_ref, sum_ref):
+def near_kernel(parts_ref, bias_ref, back_ref, sum_ref, back_out_ref):
+    back_out_ref[...] = back_ref[...]
     total = parts_ref[0].astype(F32)
     for i in range(1, parts_ref.shape[0]):
         total = total + parts_ref[i].astype(F32)
@@ -257,13 +259,20 @@
         sum_ref[i] = sums
 
 
-def far_kernel(parts_ref, sum_ref):
+def far_kernel(
+    parts_ref, own_first_ref, own_last_ref, back_ref, ev_ref, cot_ref, sum_ref, grad_ref
+):
     total = parts_ref[0].astype(F32)
     for i in range(1, parts_ref.shape[0]):
         total = total + parts_ref[i].astype(F32)
     sums = total.astype(BF16)
     for i in range(sum_ref.shape[0]):
         sum_ref[i] = sums
+    window = back_ref.shape[0]
+    for half, grad in enumerate((own_first_ref[...], own_last_ref[...] + back_ref[...])):
+        here = slice(half * window, (half + 1) * window)
+        hat, inv = norm_rows(ev_ref[here, :].astype(F32))
+        grad_ref[here, :] = (cot_ref[here, :].astype(F32) + norm_back(grad, hat, inv)).astype(BF16)
 
 
 def unpack_kernel(all_ref, w_in_ref, b_in_ref, w_out_ref):
@@ -277,14 +286,6 @@
         w_out_ref[here, half * 128 : (half + 1) * 128] = tiles[4]
         bias = tiles[5] if bias is None else bias + tiles[5]
     b_in_ref[...] = bias
-
-
-def grad_kernel(own_first_ref, own_last_ref, back_ref, ev_ref, cot_ref, grad_ref):
-    window = back_ref.shape[0]
-    for half, grad in enumerate((own_first_ref[...], own_last_ref[...] + back_ref[...])):
-        here = slice(half * window, (half + 1) * window)
-        hat, inv = norm_rows(ev_ref[here, :].astype(F32))
-        grad_ref[here, :] = (cot_ref[here, :].astype(F32) + norm_back(grad, hat, inv)).astype(BF16)
 
 
 def call(kernel, outs, *args, spaces=None, scratch=(), flops=0, moved=0):
@@ -350,15 +351,19 @@
         spaces=[pltpu.SMEM] + [pltpu.VMEM] * 14,
         flops=10**9, moved=10**7,
     )
+    parts = lax.all_to_all(parts, NEAR, 0, 0)
+    sums, back = call(
+        near_kernel,
+        [((far, PIECE + GROUP, 128), BF16, KEPT), (half, F32, KEPT)],
+        parts, bias_part, back,
+    )
     back = lax.ppermute(back, SEQ, [(i, i - 1) for i in range(1, slabs)])
-    parts = lax.all_to_all(parts, NEAR, 0, 0)
-    (grad_events,) = call(
-        grad_kernel, [((rows, width), BF16)], own_first, own_last, back, ev, cot,
-        flops=10**7, moved=10**6,
-    )
-    (sums,) = call(near_kernel, [((far, PIECE + GROUP, 128), BF16)], parts, bias_part)
     sums = lax.all_to_all(sums, FAR, 0, 0)
-    (sums,) = call(far_kernel, [((near, PIECE + GROUP, 128), BF16)], sums)
+    sums, grad_events = call(
+        far_kernel,
+        [((near, PIECE + GROUP, 128), BF16, KEPT), ((rows, width), BF16)],
+        sums, own_first, own_last, back, ev, cot,
+    )
     sums = lax.all_to_all(sums, NEAR, 0, 0)
     sum_in, sum_bias, sum_out = call(
         unpack_kernel, [((width, 4 * width), F32), ((8, 128), F32), ((width, width), F32)], sums

time: 85 us -> 85.7 us (level)
  starting transfers between devices: 13.5 us -> 20.6 us
  blocking collectives: 48.7 us -> 42.9 us
    all_to_all x1, starting transfers between devices: 6.67 us -> 13.9 us  [on_device(): sums = lax.all_to_all(sums, FAR, 0, 0)]
    all_to_all x1, blocking collectives: 26.9 us -> 21 us  [on_device(): sums = lax.all_to_all(sums, NEAR, 0, 0)]
    ppermute x1, waiting for transfers between devices: 9.93 us -> 4.36 us  [on_device(): back = lax.ppermute(back, SEQ, [(i, i - 1) for i in range(1, slabs)])]
    all_to_all x1, waiting for transfers between devices: 1.33 us -> 6.6 us  [on_device(): sums = lax.all_to_all(sums, FAR, 0, 0)]
    pallas_call x6 -> x5, Pallas kernels: 9.69 us -> 9.44 us  [call(): pl.pallas_call(kernel, out_shape=[pltpu.VMEM(shape, kind) if kept else ja...]
  transfers between devices with their start and end apart: 3 -> 3, of which waited for: 3 -> 3; matrix products, arithmetic and copies ran while one was open for 0% -> 0% of each run, Pallas kernels for 6% -> 5%
where the time goes in v3:
time: 85.7 us; the launch traced here: 85.3 us
  blocking collectives  42.9 us (50%)
  starting transfers between devices  20.6 us (24%)
  waiting for transfers between devices  11.1 us (13%)
  Pallas kernels  9.44 us (11%)
  between operations  1.31 us (2%)
    all_to_all x1, blocking collectives, on_device(): parts = lax.all_to_all(parts, NEAR, 0, 0)  21.9 us
    all_to_all x1, blocking collectives, on_device(): sums = lax.all_to_all(sums, NEAR, 0, 0)  21 us
    all_to_all x1, starting transfers between devices, on_device(): sums = lax.all_to_all(sums, FAR, 0, 0)  13.9 us
    pallas_call x5, Pallas kernels, call(): pl.pallas_call(kernel, out_shape=[pltpu.VMEM(shape, kind) if kept else ja...  9.44 us
    all_to_all x1, waiting for transfers between devices, on_device(): sums = lax.all_to_all(sums, FAR, 0, 0)  6.6 us
    ppermute x1, starting transfers between devices, on_device(): moved = lax.ppermute(events, SEQ, [(i, i + 1) for i in range(slabs - 1)])  4.51 us
    ppermute x1, waiting for transfers between devices, on_device(): back = lax.ppermute(back, SEQ, [(i, i - 1) for i in range(1, slabs)])  4.36 us
    ppermute x1, starting transfers between devices, on_device(): back = lax.ppermute(back, SEQ, [(i, i - 1) for i in range(1, slabs)])  2.2 us
  transfers between devices with their start and end apart: 3, of which 3 were waited for; matrix products, arithmetic and copies ran while one was open for 0% of the time, Pallas kernels for 5%

profile of v3, /device:TPU:1, one launch (start us, length us, event | category | flops | bytes accessed | tf_op | source)
XLA Modules:
  0.0 85.3 jit_solution(13737593014876897872)
XLA Ops:
  0.6 4.5 %collective-permute-start = (bf16[1,256,256]{2,1,0:T(8,128)(2,1)}, bf16[1,256,256]{2,1,0:T(8,128)(2,1)S(1)}, u32[]{:S(2)}, u32[]{:S(2)}) collective-permute-start(bf16[1,256,256]{2,1,0:T(8,128)(2,1)} %param.9), channel_id=1, source_target_pairs={{0,1},{1,2},{2,3},{3,4},{4,5},{5,6},{6,7},{7,8},{8,9},{9,10},{10,1... | collective-permute-start | bytes 393224 | tf_op jit(solution)/shard_map/ppermute | solution.py:319
  5.8 3.9 %shard_map.128 = (bf16[128,256]{1,0:T(8,128)(2,1)S(1)}, bf16[128,256]{1,0:T(8,128)(2,1)S(1)}, bf16[128,1024]{1,0:T(8,128)(2,1)S(1)}, f32[128,256]{1,0:T(8,128)S(...) custom-call(s32[1]{0:T(128)S(6)} %copy.14.length_ref, ...), custom_call_target="tpu_custom_call" | custom-call | flops 1000000000 | bytes 10000000 | tf_op jit(solution)/shard_map/pallas_call | solution.py:297
  9.8 0.1 collective-permute-done.moved_ref
  9.8 2.6 %shard_map.129 = (bf16[256,256]{1,0:T(8,128)(2,1)}, bf16[64,40,128]{2,1,0:T(8,128)(2,1)S(1)}, f32[8,128]{1,0:T(8,128)S(1)}, f32[128,256]{1,0:T(8,128)S(1)}, f32[128,256]{1,0:T(8,128)S(1)}) custom-call(s32[1]{0:T(128)S(6)} %copy.14.length_ref, bf16[1,256,256]{2,1,0:T(8,128)(2,1)S(1)} %collective-permute-done.moved_ref, ...), custom_call_target="tpu_custom_call" | custom-call | flops 1000000000 | bytes 10000000 | tf_op jit(solution)/shard_map/pallas_call | solution.py:297
  12.4 21.9 %all_to_all.15.parts_ref = bf16[64,40,128]{2,1,0:T(8,128)(2,1)S(1)} all-to-all(bf16[64,40,128]{2,1,0:T(8,128)(2,1)S(1)} %get-tuple-element.45), channel_id=1, replica_groups=mesh['yl'=2,'zh'=8,'zl'=2,'yh'=2,'x'=4,'c'=2] {'yl','yh','x','c','zl'}, dimensions={0} | all-to-all | bytes 1310720 | tf_op jit(solution)/shard_map/all_to_all | solution.py:354
  34.3 0.8 shard_map.130
  35.1 13.9 %all-to-all-start.1 = ((bf16[8,48,128]{2,1,0:T(8,128)(2,1)}), bf16[8,48,128]{2,1,0:T(8,128)(2,1)S(1)}, u32[]{:S(2)}, u32[]{:S(2)}) async-start(bf16[8,48,128]{2,1,0:T(8,128)(2,1)} %get-tuple-element.48), calls=%async_computation.1 | async-start | bytes 196608 | tf_op jit(solution)/shard_map/all_to_all | solution.py:361
  49.0 2.2 %collective-permute-start.1 = (f32[128,256]{1,0:T(8,128)S(1)}, f32[128,256]{1,0:T(8,128)S(1)}, u32[]{:S(2)}, u32[]{:S(2)}) collective-permute-start(f32[128,256]{1,0:T(8,128)S(1)} %get-tuple-element.51), channel_id=1, source_target_pairs={{1,0},{2,1},{3,2},{4,3},{5,4},{6,5},{7,6},{8,7},{9,8},{10,9},{11,1... | collective-permute-start | bytes 393224 | tf_op jit(solution)/shard_map/ppermute | solution.py:360
  51.2 4.4 %collective-permute-done.1.back_ref = f32[128,256]{1,0:T(8,128)S(1)} collective-permute-done((f32[128,256]{1,0:T(8,128)S(1)}, f32[128,256]{1,0:T(8,128)S(1)}, u32[]{:S(2)}, u32[]{:S(2)}) %collective-permute-start.1) | collective-permute-done | bytes 131104 | tf_op jit(solution)/shard_map/ppermute | solution.py:360
  55.6 6.6 %all-to-all-done.1.parts_ref = bf16[8,48,128]{2,1,0:T(8,128)(2,1)S(1)} async-done(((bf16[8,48,128]{2,1,0:T(8,128)(2,1)}), bf16[8,48,128]{2,1,0:T(8,128)(2,1)S(1)}, u32[]{:S(2)}, u32[]{:S(2)}) %all-to-all-start.1) | async-done | bytes 98336 | tf_op jit(solution)/shard_map/all_to_all | solution.py:361
  62.2 1.0 %shard_map.131 = (bf16[64,48,128]{2,1,0:T(8,128)(2,1)S(1)}, bf16[256,256]{1,0:T(8,128)(2,1)}) custom-call(bf16[8,48,128]{2,1,0:T(8,128)(2,1)S(1)} %all-to-all-done.1.parts_ref, f32[128,256]{1,0:T(8,128)S(1)} %get-tuple-element.49.own_first_ref, f32[128,256]{1,0:T(8,128)S(1)} %get-tuple-element.50.own_last_ref, ...), custom_call_target="tpu_custom_call" | custom-call | tf_op jit(solution)/shard_map/pallas_call | solution.py:297
  63.1 21.0 %all_to_all.16.all_ref = bf16[64,48,128]{2,1,0:T(8,128)(2,1)S(1)} all-to-all(bf16[64,48,128]{2,1,0:T(8,128)(2,1)S(1)} %get-tuple-element.53), channel_id=1, replica_groups=mesh['yl'=2,'zh'=8,'zl'=2,'yh'=2,'x'=4,'c'=2] {'yl','yh','x','c','zl'}, dimensions={0} | all-to-all | bytes 1572864 | tf_op jit(solution)/shard_map/all_to_all | solution.py:367
  84.2 1.1 %shard_map.132 = (f32[256,1024]{1,0:T(8,128)}, f32[8,128]{1,0:T(8,128)}, f32[256,256]{1,0:T(8,128)}) custom-call(bf16[64,48,128]{2,1,0:T(8,128)(2,1)S(1)} %all_to_all.16.all_ref), custom_call_target="tpu_custom_call" | custom-call | tf_op jit(solution)/shard_map/pallas_call | solution.py:297
Async XLA Ops:
  0.6 9.2 %collective-permute-start = (bf16[1,256,256]{2,1,0:T(8,128)(2,1)}, bf16[1,256,256]{2,1,0:T(8,128)(2,1)S(1)}, u32[]{:S(2)}, u32[]{:S(2)}) collective-permute-start(bf16[1,256,256]{2,1,0:T(8,128)(2,1)} %param.9), channel_id=1, source_target_pairs={{0,1},{1,2},{2,3},{3,4},{4,5},{5,6},{6,7},{7,8},{8,9},{9,10},{10,1... | collective-permute-start | bytes 393224 | tf_op jit(solution)/shard_map/ppermute | solution.py:319
  35.1 27.1 %all-to-all-start.1 = ((bf16[8,48,128]{2,1,0:T(8,128)(2,1)}), bf16[8,48,128]{2,1,0:T(8,128)(2,1)S(1)}, u32[]{:S(2)}, u32[]{:S(2)}) async-start(bf16[8,48,128]{2,1,0:T(8,128)(2,1)} %get-tuple-element.48), calls=%async_computation.1 | async-start | bytes 196608 | tf_op jit(solution)/shard_map/all_to_all | solution.py:361
  49.0 6.6 %collective-permute-start.1 = (f32[128,256]{1,0:T(8,128)S(1)}, f32[128,256]{1,0:T(8,128)S(1)}, u32[]{:S(2)}, u32[]{:S(2)}) collective-permute-start(f32[128,256]{1,0:T(8,128)S(1)} %get-tuple-element.51), channel_id=1, source_target_pairs={{1,0},{2,1},{3,2},{4,3},{5,4},{6,5},{7,6},{8,7},{9,8},{10,9},{11,1... | collective-permute-start | bytes 393224 | tf_op jit(solution)/shard_map/ppermute | solution.py:360

commit v4 on v2

--- a/solution.py
+++ b/solution.py
@@ -16,7 +16,10 @@
 BATCH = ("yl", "zh", "zl")
 SEQ = ("yh", "x", "c")
 GROUP = 8
-PIECE = 5 * GROUP
+PIECE = 6 * GROUP
+BACK = 4
+NEAR_FIRST = 48
+KEPT = True
 
 
 def norm_rows(values):
@@ -174,7 +177,7 @@
 def edge_kernel(
     scale, length_ref, moved_ref, out_last_ref, gated_ref, pre_ref, normed_ref, proj_ref,
     slope_ref, bias_ref, grads_ref, ev_ref, cot_ref, w_in_ref, b_in_ref, w_out_ref,
-    out_ref, parts_ref, bias_out_ref, own_ref, back_ref,
+    out_ref, parts_ref, own_ref,
 ):
     rows, width = ev_ref.shape
     window = out_last_ref.shape[0]
@@ -231,43 +234,58 @@
         in_blocks.append(dot(left[: right.shape[0]], right, COLS_BY_COLS) * scale)
         bias_rows.append(jnp.sum(right.astype(F32), axis=0, keepdims=True) * scale)
     own_ref[...] = own_total
-    back_ref[...] = back_total
     part_out = dot(
         jnp.concatenate([gated, gated_ref[...]], axis=0), cot_ref[...], COLS_BY_COLS
     ) * scale
-    for i in range(8):
-        bias_out_ref[i : i + 1, :] = bias_rows[i // 2][:, (i % 2) * 128 : (i % 2 + 1) * 128]
-    for group in range(width // GROUP):
+    tile_row = lax.broadcasted_iota(jnp.int32, (GROUP, 128), 0)
+    for piece in range(parts_ref.shape[0]):
+        group, half = piece // 2, piece % 2
         here = slice(group * GROUP, (group + 1) * GROUP)
-        for half in range(2):
-            tiles = [
-                in_blocks[2 * half + k // 2][here, (k % 2) * 128 : (k % 2 + 1) * 128]
-                for k in range(4)
-            ]
-            tiles.append(part_out[here, half * 128 : (half + 1) * 128])
-            parts_ref[2 * group + half] = jnp.concatenate(tiles, axis=0).astype(BF16)
-
-
-def near_kernel(parts_ref, bias_ref, sum_ref):
+        tiles = [
+            in_blocks[2 * half + k // 2][here, (k % 2) * 128 : (k % 2 + 1) * 128]
+            for k in range(4)
+        ]
+        tiles.append(part_out[here, half * 128 : (half + 1) * 128])
+        rest = back_total[
+            piece // 4 * GROUP : (piece // 4 + 1) * GROUP,
+            piece // 2 % 2 * 128 : (piece // 2 % 2 + 1) * 128,
+        ]
+        if piece % 2:
+            rest = pltpu.roll(rest, BACK, 0)
+        line = piece // 8
+        bias = bias_rows[line // 2][:, line % 2 * 128 : (line % 2 + 1) * 128]
+        tiles.append(jnp.where(tile_row < BACK, rest, jnp.broadcast_to(bias, (GROUP, 128))))
+        parts_ref[piece] = jnp.concatenate(tiles, axis=0).astype(BF16)
+
+
+def near_kernel(parts_ref, sum_ref, back_ref):
+    total = None
+    for i in range(parts_ref.shape[0]):
+        piece = parts_ref[i].astype(F32)
+        back_ref[i] = piece[5 * GROUP :]
+        total = piece if total is None else total + piece
+    sums = total.astype(BF16)
+    for i in range(sum_ref.shape[0]):
+        sum_ref[i] = sums
+
+
+def far_kernel(sources, parts_ref, back_ref, sum_ref):
     total = parts_ref[0].astype(F32)
     for i in range(1, parts_ref.shape[0]):
         total = total + parts_ref[i].astype(F32)
-    sums = jnp.concatenate([total, bias_ref[...]], axis=0).astype(BF16)
-    for i in range(sum_ref.shape[0]):
-        sum_ref[i] = sums
-
-
-def far_kernel(parts_ref, sum_ref):
-    total = parts_ref[0].astype(F32)
-    for i in range(1, parts_ref.shape[0]):
-        total = total + parts_ref[i].astype(F32)
-    sums = total.astype(BF16)
-    for i in range(sum_ref.shape[0]):
-        sum_ref[i] = sums
-
-
-def unpack_kernel(all_ref, w_in_ref, b_in_ref, w_out_ref):
-    bias = None
+    tile_row = lax.broadcasted_iota(jnp.int32, (GROUP, 128), 0)
+    rest = total[5 * GROUP :]
+    for i, source in enumerate(sources):
+        back = jnp.zeros_like(rest) if source is None else back_ref[source]
+        last = jnp.where(tile_row < BACK, back, rest)
+        sum_ref[i] = jnp.concatenate([total[: 5 * GROUP], last], axis=0).astype(BF16)
+
+
+def unpack_kernel(
+    all_ref, own_first_ref, own_last_ref, ev_ref, cot_ref, w_in_ref, b_in_ref, w_out_ref, grad_ref
+):
+    tile_row = lax.broadcasted_iota(jnp.int32, (GROUP, 128), 0)
+    lasts = []
     for piece in range(all_ref.shape[0]):
         rows = all_ref[piece].astype(F32)
         group, half = piece // 2, piece % 2
@@ -275,13 +293,24 @@
         tiles = [rows[k * GROUP : (k + 1) * GROUP] for k in range(6)]
         w_in_ref[here, half * 512 : (half + 1) * 512] = jnp.concatenate(tiles[:4], axis=1)
         w_out_ref[here, half * 128 : (half + 1) * 128] = tiles[4]
-        bias = tiles[5] if bias is None else bias + tiles[5]
-    b_in_ref[...] = bias
-
-
-def grad_kernel(own_first_ref, own_last_ref, back_ref, ev_ref, cot_ref, grad_ref):
-    window = back_ref.shape[0]
-    for half, grad in enumerate((own_first_ref[...], own_last_ref[...] + back_ref[...])):
+        if piece % 8 == 0:
+            b_in_ref[piece // 8 : piece // 8 + 1, :] = tiles[5][BACK : BACK + 1]
+        lasts.append(tiles[5])
+    back = jnp.concatenate(
+        [
+            jnp.concatenate(
+                [
+                    jnp.where(tile_row < BACK, lasts[i], pltpu.roll(lasts[i + 1], BACK, 0))
+                    for i in (4 * t, 4 * t + 2)
+                ],
+                axis=1,
+            )
+            for t in range(len(lasts) // 4)
+        ],
+        axis=0,
+    )
+    window = back.shape[0]
+    for half, grad in enumerate((own_first_ref[...], own_last_ref[...] + back)):
         here = slice(half * window, (half + 1) * window)
         hat, inv = norm_rows(ev_ref[here, :].astype(F32))
         grad_ref[here, :] = (cot_ref[here, :].astype(F32) + norm_back(grad, hat, inv)).astype(BF16)
@@ -339,29 +368,37 @@
         ],
         flops=10**9, moved=10**7,
     )
-    layer_out, parts, bias_part, own_first, back = call(
+    layer_out, parts, own_first = call(
         functools.partial(edge_kernel, scale),
-        [
-            ((rows, width), BF16), ((near, PIECE, 128), BF16), ((8, 128), F32), (half, F32),
-            (half, F32),
-        ],
+        [((rows, width), BF16), ((near, PIECE, 128), BF16, KEPT), (half, F32, KEPT)],
         history_lengths, moved, out_last, gated, pre, normed, proj, slope, bias, grads, ev, cot,
         w_in_near, b_in_near, w_out_near,
         spaces=[pltpu.SMEM] + [pltpu.VMEM] * 14,
         flops=10**9, moved=10**7,
     )
-    back = lax.ppermute(back, SEQ, [(i, i - 1) for i in range(1, slabs)])
-    parts = lax.all_to_all(parts, NEAR, 0, 0)
-    (grad_events,) = call(
-        grad_kernel, [((rows, width), BF16)], own_first, own_last, back, ev, cot,
-        flops=10**7, moved=10**6,
-    )
-    (sums,) = call(near_kernel, [((far, PIECE + GROUP, 128), BF16)], parts, bias_part)
-    sums = lax.all_to_all(sums, FAR, 0, 0)
-    (sums,) = call(far_kernel, [((near, PIECE + GROUP, 128), BF16)], sums)
-    sums = lax.all_to_all(sums, NEAR, 0, 0)
-    sum_in, sum_bias, sum_out = call(
-        unpack_kernel, [((width, 4 * width), F32), ((8, 128), F32), ((width, width), F32)], sums
+    zl = lax.axis_size("zl")
+    order = [(i + NEAR_FIRST) % near for i in range(near)]
+    sources = [
+        order.index(i + zl) if i // zl % slabs < slabs - 1 else None for i in order
+    ]
+    parts = lax.all_to_all(parts, NEAR, 0, 0, axis_index_groups=[order])
+    sums, back = call(
+        near_kernel, [((far, PIECE, 128), BF16, KEPT), ((near, GROUP, 128), F32, KEPT)], parts
+    )
+    sums = lax.all_to_all(
+        sums, FAR, 0, 0, axis_index_groups=[[(i + far // 2) % far for i in range(far)]]
+    )
+    (sums,) = call(
+        functools.partial(far_kernel, sources), [((near, PIECE, 128), BF16, KEPT)], sums, back
+    )
+    sums = lax.all_to_all(sums, NEAR, 0, 0, axis_index_groups=[order])
+    sum_in, sum_bias, sum_out, grad_events = call(
+        unpack_kernel,
+        [
+            ((width, 4 * width), F32), ((8, 128), F32), ((width, width), F32),
+            ((rows, width), BF16),
+        ],
+        sums, own_first, own_last, ev, cot,
     )
     return (layer_out[None], grad_events[None], sum_in, sum_bias.reshape(4 * width), sum_out)
 

time: 85 us -> 79.3 us (0.933)
  blocking collectives: 48.7 us -> 65.1 us
  waiting for transfers between devices: 11.4 us -> 0.1 us
  starting transfers between devices: 13.5 us -> 4.51 us
  Pallas kernels: 9.69 us -> 8.06 us
    all_to_all x2 -> x3, blocking collectives: 48.7 us -> 65.1 us  [the longest x1 23 us: on_device(): parts = lax.all_to_all(parts, NEAR, 0, 0, axis_index_groups=[order])]
    ppermute x1 -> x0, waiting for transfers between devices: 9.93 us -> none  [on_device(): back = lax.ppermute(back, SEQ, [(i, i - 1) for i in range(1, slabs)])]
    all_to_all x1 -> x0, starting transfers between devices: 6.67 us -> none  [on_device(): sums = lax.all_to_all(sums, NEAR, 0, 0)]
    ppermute x1 -> x0, starting transfers between devices: 2.36 us -> none  [on_device(): back = lax.ppermute(back, SEQ, [(i, i - 1) for i in range(1, slabs)])]
    pallas_call x6 -> x5, Pallas kernels: 9.69 us -> 8.06 us  [call(): pl.pallas_call(kernel, out_shape=[pltpu.VMEM(shape, kind) if kept else ja...]
    all_to_all x1 -> x0, waiting for transfers between devices: 1.33 us -> none  [on_device(): sums = lax.all_to_all(sums, NEAR, 0, 0)]
  transfers between devices with their start and end apart: 3 -> 1, of which waited for: 3 -> 1; matrix products, arithmetic and copies ran while one was open for 0% -> 0% of each run, Pallas kernels for 6% -> 5%
where the time goes in v4:
time: 79.3 us; the launch traced here: 79.1 us
  blocking collectives  65.1 us (82%)
  Pallas kernels  8.06 us (10%)
  starting transfers between devices  4.51 us (6%)
  between operations  1.3 us (2%)
    all_to_all x1, blocking collectives, on_device(): parts = lax.all_to_all(parts, NEAR, 0, 0, axis_index_groups=[order])  23 us
    all_to_all x1, blocking collectives, on_device(): lax.all_to_all(sums, FAR, 0, 0, axis_index_groups=[[(i + far // 2) % far...  21.3 us
    all_to_all x1, blocking collectives, on_device(): sums = lax.all_to_all(sums, NEAR, 0, 0, axis_index_groups=[order])  20.8 us
    pallas_call x5, Pallas kernels, call(): pl.pallas_call(kernel, out_shape=[pltpu.VMEM(shape, kind) if kept else ja...  8.06 us
    ppermute x1, starting transfers between devices, on_device(): moved = lax.ppermute(events, SEQ, [(i, i + 1) for i in range(slabs - 1)])  4.51 us
  transfers between devices with their start and end apart: 1, of which 1 were waited for; matrix products, arithmetic and copies ran while one was open for 0% of the time, Pallas kernels for 5%

profile of v4, /device:TPU:1, one launch (start us, length us, event | category | flops | bytes accessed | tf_op | source)
XLA Modules:
  0.0 79.1 jit_solution(10974777996487768439)
XLA Ops:
  0.6 4.5 %collective-permute-start = (bf16[1,256,256]{2,1,0:T(8,128)(2,1)}, bf16[1,256,256]{2,1,0:T(8,128)(2,1)S(1)}, u32[]{:S(2)}, u32[]{:S(2)}) collective-permute-start(bf16[1,256,256]{2,1,0:T(8,128)(2,1)} %param.9), channel_id=1, source_target_pairs={{0,1},{1,2},{2,3},{3,4},{4,5},{5,6},{6,7},{7,8},{8,9},{9,10},{10,1... | collective-permute-start | bytes 393224 | tf_op jit(solution)/shard_map/ppermute | solution.py:347
  5.8 3.9 %shard_map.128 = (bf16[128,256]{1,0:T(8,128)(2,1)S(1)}, bf16[128,256]{1,0:T(8,128)(2,1)S(1)}, bf16[128,1024]{1,0:T(8,128)(2,1)S(1)}, f32[128,256]{1,0:T(8,128)S(...) custom-call(s32[1]{0:T(128)S(6)} %copy.14.length_ref, ...), custom_call_target="tpu_custom_call" | custom-call | flops 1000000000 | bytes 10000000 | tf_op jit(solution)/shard_map/pallas_call | solution.py:325
  9.7 0.1 collective-permute-done.moved_ref
  9.8 2.6 %shard_map.129 = (bf16[256,256]{1,0:T(8,128)(2,1)}, bf16[64,48,128]{2,1,0:T(8,128)(2,1)S(1)}, f32[128,256]{1,0:T(8,128)S(1)}) custom-call(s32[1]{0:T(128)S(6)} %copy.14.length_ref, bf16[1,256,256]{2,1,0:T(8,128)(2,1)S(1)} %collective-permute-done.moved_ref, bf16[128,256]{1,0:T(8,128)(2,1)S(1)} %get-tuple-element.28.out_last_ref, ...), custom_call_target="tpu_custom_call" | custom-call | flops 1000000000 | bytes 10000000 | tf_op jit(solution)/shard_map/pallas_call | solution.py:325
  12.4 23.0 %all_to_all.15.parts_ref = bf16[64,48,128]{2,1,0:T(8,128)(2,1)S(1)} all-to-all(bf16[64,48,128]{2,1,0:T(8,128)(2,1)S(1)} %get-tuple-element.42), channel_id=1, replica_groups={{264,280,265,281,266,282,267,283,268,284,269,285,270,286,271,287,0,16,1..., dimensions={0} | all-to-all | bytes 1572864 | tf_op jit(solution)/shard_map/all_to_all | solution.py:384
  35.4 0.1 shard_map.130
  35.5 21.3 %all_to_all.16.parts_ref = bf16[8,48,128]{2,1,0:T(8,128)(2,1)S(1)} all-to-all(bf16[8,48,128]{2,1,0:T(8,128)(2,1)S(1)} %get-tuple-element.43), channel_id=1, replica_groups={{128,160,192,224,0,32,64,96},{129,161,193,225,1,33,65,97},{130,162,194,..., dimensions={0} | all-to-all | bytes 196608 | tf_op jit(solution)/shard_map/all_to_all | solution.py:388
  56.9 0.1 shard_map.131
  56.9 20.8 %all_to_all.17.all_ref = bf16[64,48,128]{2,1,0:T(8,128)(2,1)S(1)} all-to-all(bf16[64,48,128]{2,1,0:T(8,128)(2,1)S(1)} %shard_map.131), channel_id=1, replica_groups={{264,280,265,281,266,282,267,283,268,284,269,285,270,286,271,287,0,16,1..., dimensions={0} | all-to-all | bytes 1572864 | tf_op jit(solution)/shard_map/all_to_all | solution.py:394
  77.7 1.3 %shard_map.132 = (f32[256,1024]{1,0:T(8,128)}, f32[8,128]{1,0:T(8,128)}, f32[256,256]{1,0:T(8,128)}, bf16[256,256]{1,0:T(8,128)(2,1)}) custom-call(bf16[64,48,128]{2,1,0:T(8,128)(2,1)S(1)} %all_to_all.17.all_ref, f32[128,256]{1,0:T(8,128)S(1)} %get-tuple-element.45.own_first_ref, f32[128,256]{1,0:T(8,128)S(1)} %get-tuple-element.46.own_last_ref, ...), custom_call_target="tpu_custom_call" | custom-call | tf_op jit(solution)/shard_map/pallas_call | solution.py:325
Async XLA Ops:
  0.6 9.2 %collective-permute-start = (bf16[1,256,256]{2,1,0:T(8,128)(2,1)}, bf16[1,256,256]{2,1,0:T(8,128)(2,1)S(1)}, u32[]{:S(2)}, u32[]{:S(2)}) collective-permute-start(bf16[1,256,256]{2,1,0:T(8,128)(2,1)} %param.9), channel_id=1, source_target_pairs={{0,1},{1,2},{2,3},{3,4},{4,5},{5,6},{6,7},{7,8},{8,9},{9,10},{10,1... | collective-permute-start | bytes 393224 | tf_op jit(solution)/shard_map/ppermute | solution.py:347

commit v5 on v4

--- a/solution.py
+++ b/solution.py
@@ -18,8 +18,10 @@
 GROUP = 8
 PIECE = 6 * GROUP
 BACK = 4
-NEAR_FIRST = 48
-KEPT = True
+PARTS = 4
+NEAR_FIRST = 24
+KEPT = pltpu.VMEM
+SENT = pltpu.HBM
 
 
 def norm_rows(values):
@@ -282,11 +284,23 @@
 
 
 def unpack_kernel(
-    all_ref, own_first_ref, own_last_ref, ev_ref, cot_ref, w_in_ref, b_in_ref, w_out_ref, grad_ref
+    all_ref, own_first_ref, own_last_ref, ev_ref, cot_ref, out_ref,
+    w_in_hbm, b_in_hbm, w_out_hbm, grad_hbm, out_hbm,
+    w_in_ref, b_in_ref, w_out_ref, grad_ref, sems,
 ):
+    copies = []
+
+    def send(source, target):
+        copy = pltpu.make_async_copy(source, target, sems.at[len(copies)])
+        copy.start()
+        copies.append(copy)
+
+    send(out_ref, out_hbm)
     tile_row = lax.broadcasted_iota(jnp.int32, (GROUP, 128), 0)
     lasts = []
-    for piece in range(all_ref.shape[0]):
+    pieces = all_ref.shape[0]
+    part = pieces // PARTS
+    for piece in range(pieces):
         rows = all_ref[piece].astype(F32)
         group, half = piece // 2, piece % 2
         here = slice(group * GROUP, (group + 1) * GROUP)
@@ -296,6 +310,11 @@
         if piece % 8 == 0:
             b_in_ref[piece // 8 : piece // 8 + 1, :] = tiles[5][BACK : BACK + 1]
         lasts.append(tiles[5])
+        if (piece + 1) % part == 0:
+            done = pl.ds((piece + 1 - part) // 2 * GROUP, part // 2 * GROUP)
+            send(w_in_ref.at[done], w_in_hbm.at[done])
+    send(w_out_ref, w_out_hbm)
+    send(b_in_ref, b_in_hbm)
     back = jnp.concatenate(
         [
             jnp.concatenate(
@@ -314,6 +333,9 @@
         here = slice(half * window, (half + 1) * window)
         hat, inv = norm_rows(ev_ref[here, :].astype(F32))
         grad_ref[here, :] = (cot_ref[here, :].astype(F32) + norm_back(grad, hat, inv)).astype(BF16)
+    send(grad_ref, grad_hbm)
+    for copy in copies:
+        copy.wait()
 
 
 def call(kernel, outs, *args, spaces=None, scratch=(), flops=0, moved=0):
@@ -325,11 +347,14 @@
     return pl.pallas_call(
         kernel,
         out_shape=[
-            pltpu.VMEM(shape, kind) if kept else jax.ShapeDtypeStruct(shape, kind)
-            for shape, kind, *kept in outs
+            pltpu.VMEM(shape, kind) if KEPT in place else jax.ShapeDtypeStruct(shape, kind)
+            for shape, kind, *place in outs
         ],
         in_specs=[pl.BlockSpec(memory_space=space) for space in spaces],
-        out_specs=[pl.BlockSpec(memory_space=pltpu.VMEM)] * len(outs),
+        out_specs=[
+            pl.BlockSpec(memory_space=SENT if SENT in place else pltpu.VMEM)
+            for _, _, *place in outs
+        ],
         scratch_shapes=scratch,
         compiler_params=pltpu.CompilerParams(vmem_limit_bytes=24 * 1024 * 1024),
         cost_estimate=pl.CostEstimate(flops=flops, bytes_accessed=moved, transcendentals=0),
@@ -370,7 +395,7 @@
     )
     layer_out, parts, own_first = call(
         functools.partial(edge_kernel, scale),
-        [((rows, width), BF16), ((near, PIECE, 128), BF16, KEPT), (half, F32, KEPT)],
+        [((rows, width), BF16, KEPT), ((near, PIECE, 128), BF16, KEPT), (half, F32, KEPT)],
         history_lengths, moved, out_last, gated, pre, normed, proj, slope, bias, grads, ev, cot,
         w_in_near, b_in_near, w_out_near,
         spaces=[pltpu.SMEM] + [pltpu.VMEM] * 14,
@@ -386,19 +411,24 @@
         near_kernel, [((far, PIECE, 128), BF16, KEPT), ((near, GROUP, 128), F32, KEPT)], parts
     )
     sums = lax.all_to_all(
-        sums, FAR, 0, 0, axis_index_groups=[[(i + far // 2) % far for i in range(far)]]
+        sums, FAR, 0, 0, axis_index_groups=[[(i + 5) % far for i in range(far)]]
     )
     (sums,) = call(
         functools.partial(far_kernel, sources), [((near, PIECE, 128), BF16, KEPT)], sums, back
     )
     sums = lax.all_to_all(sums, NEAR, 0, 0, axis_index_groups=[order])
-    sum_in, sum_bias, sum_out, grad_events = call(
+    sum_in, sum_bias, sum_out, grad_events, layer_out = call(
         unpack_kernel,
         [
-            ((width, 4 * width), F32), ((8, 128), F32), ((width, width), F32),
-            ((rows, width), BF16),
-        ],
-        sums, own_first, own_last, ev, cot,
+            ((width, 4 * width), F32, SENT), ((8, 128), F32, SENT), ((width, width), F32, SENT),
+            ((rows, width), BF16, SENT), ((rows, width), BF16, SENT),
+        ],
+        sums, own_first, own_last, ev, cot, layer_out,
+        scratch=[
+            pltpu.VMEM((width, 4 * width), F32), pltpu.VMEM((8, 128), F32),
+            pltpu.VMEM((width, width), F32), pltpu.VMEM((rows, width), BF16),
+            pltpu.SemaphoreType.DMA((PARTS + 4,)),
+        ],
     )
     return (layer_out[None], grad_events[None], sum_in, sum_bias.reshape(4 * width), sum_out)
 

time: 79.3 us -> 77.2 us (0.974)
  blocking collectives: 65.1 us -> 63.5 us
    all_to_all x1, blocking collectives: 20.8 us -> 18.9 us  [on_device(): sums = lax.all_to_all(sums, NEAR, 0, 0, axis_index_groups=[order])]
where the time goes in v5:
time: 77.2 us; the launch traced here: 77 us
  blocking collectives  63.5 us (82%)
  Pallas kernels  7.52 us (10%)
  starting transfers between devices  4.51 us (6%)
  between operations  1.31 us (2%)
    all_to_all x1, blocking collectives, on_device(): parts = lax.all_to_all(parts, NEAR, 0, 0, axis_index_groups=[order])  22.6 us
    all_to_all x1, blocking collectives, on_device(): lax.all_to_all(sums, FAR, 0, 0, axis_index_groups=[[(i + 5) % far for i i...  22 us
    all_to_all x1, blocking collectives, on_device(): sums = lax.all_to_all(sums, NEAR, 0, 0, axis_index_groups=[order])  18.9 us
    pallas_call x5, Pallas kernels, call(): pl.pallas_call(kernel, out_shape=[pltpu.VMEM(shape, kind) if KEPT in plac...  7.52 us
    ppermute x1, starting transfers between devices, on_device(): moved = lax.ppermute(events, SEQ, [(i, i + 1) for i in range(slabs - 1)])  4.51 us
  transfers between devices with their start and end apart: 1, of which 1 were waited for; matrix products, arithmetic and copies ran while one was open for 0% of the time, Pallas kernels for 5%

profile of v5, /device:TPU:1, one launch (start us, length us, event | category | flops | bytes accessed | tf_op | source)
XLA Modules:
  0.0 77.0 jit_solution(8152163360708948828)
XLA Ops:
  0.6 4.5 %collective-permute-start = (bf16[1,256,256]{2,1,0:T(8,128)(2,1)}, bf16[1,256,256]{2,1,0:T(8,128)(2,1)S(1)}, u32[]{:S(2)}, u32[]{:S(2)}) collective-permute-start(bf16[1,256,256]{2,1,0:T(8,128)(2,1)} %param.9), channel_id=1, source_target_pairs={{0,1},{1,2},{2,3},{3,4},{4,5},{5,6},{6,7},{7,8},{8,9},{9,10},{10,1... | collective-permute-start | bytes 393224 | tf_op jit(solution)/shard_map/ppermute | solution.py:372
  5.8 3.9 %shard_map.128 = (bf16[128,256]{1,0:T(8,128)(2,1)S(1)}, bf16[128,256]{1,0:T(8,128)(2,1)S(1)}, bf16[128,1024]{1,0:T(8,128)(2,1)S(1)}, f32[128,256]{1,0:T(8,128)S(...) custom-call(s32[1]{0:T(128)S(6)} %copy.14.length_ref, ...), custom_call_target="tpu_custom_call" | custom-call | flops 1000000000 | bytes 10000000 | tf_op jit(solution)/shard_map/pallas_call | solution.py:347
  9.7 0.1 collective-permute-done.moved_ref
  9.8 2.0 %shard_map.129 = (bf16[256,256]{1,0:T(8,128)(2,1)S(1)}, bf16[64,48,128]{2,1,0:T(8,128)(2,1)S(1)}, f32[128,256]{1,0:T(8,128)S(1)}) custom-call(s32[1]{0:T(128)S(6)} %copy.14.length_ref, bf16[1,256,256]{2,1,0:T(8,128)(2,1)S(1)} %collective-permute-done.moved_ref, bf16[128,256]{1,0:T(8,128)(2,1)S(1)} %get-tuple-element.29.out_last_ref, ...), custom_call_target="tpu_custom_call" | custom-call | flops 1000000000 | bytes 10000000 | tf_op jit(solution)/shard_map/pallas_call | solution.py:347
  11.8 22.6 %all_to_all.15.parts_ref = bf16[64,48,128]{2,1,0:T(8,128)(2,1)S(1)} all-to-all(bf16[64,48,128]{2,1,0:T(8,128)(2,1)S(1)} %get-tuple-element.42), channel_id=1, replica_groups={{12,28,13,29,14,30,15,31,256,272,257,273,258,274,259,275,260,276,261,27..., dimensions={0} | all-to-all | bytes 1572864 | tf_op jit(solution)/shard_map/all_to_all | solution.py:409
  34.4 0.1 shard_map.130
  34.5 22.0 %all_to_all.16.parts_ref = bf16[8,48,128]{2,1,0:T(8,128)(2,1)S(1)} all-to-all(bf16[8,48,128]{2,1,0:T(8,128)(2,1)S(1)} %get-tuple-element.43), channel_id=1, replica_groups={{160,192,224,0,32,64,96,128},{161,193,225,1,33,65,97,129},{162,194,226,..., dimensions={0} | all-to-all | bytes 196608 | tf_op jit(solution)/shard_map/all_to_all | solution.py:413
  56.6 0.1 shard_map.131
  56.6 18.9 %all_to_all.17.all_ref = bf16[64,48,128]{2,1,0:T(8,128)(2,1)S(1)} all-to-all(bf16[64,48,128]{2,1,0:T(8,128)(2,1)S(1)} %shard_map.131), channel_id=1, replica_groups={{12,28,13,29,14,30,15,31,256,272,257,273,258,274,259,275,260,276,261,27..., dimensions={0} | all-to-all | bytes 1572864 | tf_op jit(solution)/shard_map/all_to_all | solution.py:419
  75.6 1.4 %shard_map.132 = (f32[256,1024]{1,0:T(8,128)}, f32[8,128]{1,0:T(8,128)}, f32[256,256]{1,0:T(8,128)}, bf16[256,256]{1,0:T(8,128)(2,1)}, bf16[256,256]{1,0:T(8,128)(2,1)}) custom-call(bf16[64,48,128]{2,1,0:T(8,128)(2,1)S(1)} %all_to_all.17.all_ref, f32[128,256]{1,0:T(8,128)S(1)} %get-tuple-element.45.own_first_ref, ...), custom_call_target="tpu_custom_call" | custom-call | tf_op jit(solution)/shard_map/pallas_call | solution.py:347
Async XLA Ops:
  0.6 9.2 %collective-permute-start = (bf16[1,256,256]{2,1,0:T(8,128)(2,1)}, bf16[1,256,256]{2,1,0:T(8,128)(2,1)S(1)}, u32[]{:S(2)}, u32[]{:S(2)}) collective-permute-start(bf16[1,256,256]{2,1,0:T(8,128)(2,1)} %param.9), channel_id=1, source_target_pairs={{0,1},{1,2},{2,3},{3,4},{4,5},{5,6},{6,7},{7,8},{8,9},{9,10},{10,1... | collective-permute-start | bytes 393224 | tf_op jit(solution)/shard_map/ppermute | solution.py:372

commit v6 on v5

--- a/solution.py
+++ b/solution.py
@@ -124,8 +124,8 @@
 
 def own_kernel(
     length_ref, ev_hbm, cot_hbm, ids_hbm, w_in_hbm, b_in_hbm, w_out_hbm, pos_hbm, time_hbm,
-    out_ref, gated_ref, pre_ref, own_ref, normed_ref, proj_ref, slope_ref, bias_ref, grads_ref,
-    ev_ref, cot_ref, w_in_ref, b_in_ref, w_out_ref,
+    out_ref, gated_ref, pre_ref, own_ref, normed_ref, proj_ref, slope_ref, base_ref, mask_ref,
+    grads_ref, stack_ref, att_ref, ratio_ref, ev_ref, cot_ref, w_in_ref, b_in_ref, w_out_ref,
     ids_ref, pos_ref, time_ref, sems,
 ):
     pairs = [
@@ -137,7 +137,7 @@
         copy.start()
     rows, width = ev_ref.shape
     heads, window = pos_ref.shape
-    real = length_ref[0] - lax.axis_index(SEQ) * rows
+    slab = lax.axis_index(SEQ)
     band = Band(heads, window, width)
     copies[0].wait()
     hat, _ = norm_rows(ev_ref[...].astype(F32))
@@ -151,12 +151,10 @@
     proj_ref[...] = projected[first]
     slope_ref[...] = slope[first]
     gate, values, queries, keys = [projected[:, i * width : (i + 1) * width] for i in range(4)]
-    for copy in copies[3:6]:
+    for copy in copies[3:]:
         copy.wait()
-    bias_ref[...] = band.bias(ids_ref[first, :], pos_ref, time_ref)
+    real = length_ref[0] - slab * rows
     bias = band.bias(ids_ref[last, :], pos_ref, time_ref)
-    copies[6].wait()
-    copies[7].wait()
     out, gated, grad_gate, grad_values, grad_queries, grad_keys = band.block(
         queries[last],
         jnp.concatenate([keys[last], keys[first]], axis=0),
@@ -175,18 +173,34 @@
     pre_ref[...] = pre
     own_ref[...] = dot(pre, w_in_ref[...], ROWS_BY_ROWS)
 
+    stack = band.by_head(queries[first])
+    stack_ref[...] = stack
+    near = dot(stack, keys[first], ROWS_BY_ROWS) / math.sqrt(band.head)
+    bias = band.bias(ids_ref[first, :], pos_ref, time_ref)
+    base = jnp.where(band.recent, near, 0.0) + bias
+    base_ref[...] = base
+    allowed = (band.row < real) & (band.recent | (slab > 0))
+    mask = jnp.where(allowed, 1.0 / window, 0.0)
+    mask_ref[...] = mask
+    act, _ = silu_and_slope(base)
+    weights = jnp.where(band.recent, act * mask, 0.0).astype(BF16)
+    att_ref[...] = band.pick_heads(dot(weights, values[first]))
+    upstream = dot(cot_ref[first, :], w_out_ref[...], ROWS_BY_ROWS)
+    ratio_ref[:, :width] = upstream * gate[first].astype(F32)
+    ratio_ref[:, width:] = upstream * slope[first, :width]
+
 
 def edge_kernel(
-    scale, length_ref, moved_ref, out_last_ref, gated_ref, pre_ref, normed_ref, proj_ref,
-    slope_ref, bias_ref, grads_ref, ev_ref, cot_ref, w_in_ref, b_in_ref, w_out_ref,
+    scale, moved_ref, out_last_ref, gated_ref, pre_ref, normed_ref, proj_ref, slope_ref, base_ref,
+    mask_ref, grads_ref, stack_ref, att_ref, ratio_ref, ev_ref, cot_ref, w_in_ref, b_in_ref,
+    w_out_ref,
     out_ref, parts_ref, own_ref,
 ):
     rows, width = ev_ref.shape
     window = out_last_ref.shape[0]
-    heads = bias_ref.shape[0] // window
-    slab = lax.axis_index(SEQ)
-    real = length_ref[0] - slab * rows
+    heads = base_ref.shape[0] // window
     band = Band(heads, window, width)
+    root = math.sqrt(band.head)
     first, last = slice(0, window), slice(window, 2 * window)
     tail_hat, _ = norm_rows(moved_ref[0, rows - window :, :].astype(F32))
     tail_normed = tail_hat.astype(BF16)
@@ -199,23 +213,32 @@
         value, slope = silu_and_slope(pre_act)
         return (value.astype(BF16), slope)
 
+    tail_keys, tail_keys_slope = project(3)
+    stack = stack_ref[...]
+    behind = dot(stack, tail_keys, ROWS_BY_ROWS) / root
     tail_values, tail_values_slope = project(1)
-    tail_keys, tail_keys_slope = project(3)
-    gate, values, queries, keys = [proj_ref[:, columns(i)] for i in range(4)]
-    out, gated, grad_gate, grad_values, grad_queries, grad_keys = band.block(
-        queries,
-        jnp.concatenate([keys, tail_keys], axis=0),
-        jnp.concatenate([values, tail_values], axis=0),
-        gate, bias_ref[...], (band.row < real) & (band.recent | (slab > 0)),
-        ev_ref[first, :], cot_ref[first, :], w_out_ref[...],
-    )
-    out_ref[first, :] = out
+    act, slope = silu_and_slope(base_ref[...] + jnp.where(band.recent, 0.0, behind))
+    weights = band.split(act * mask_ref[...])
+    attended = att_ref[...] + band.pick_heads(dot(weights[:, window:], tail_values))
+    att_hat, att_inv = norm_rows(attended)
+    grad_att = band.by_head(
+        norm_back(ratio_ref[:, :width], att_hat, att_inv).astype(BF16)
+    )
+    pair_values = jnp.concatenate([proj_ref[:, columns(1)], tail_values], axis=0)
+    grad_weights = band.join(dot(grad_att, pair_values, ROWS_BY_ROWS))
+    grad_scores = band.split(grad_weights * slope * mask_ref[...])
+    grad_values = dot(weights, grad_att, COLS_BY_COLS)
+    pair_keys = jnp.concatenate([proj_ref[:, columns(3)], tail_keys], axis=0)
+    grad_queries = band.pick_heads(dot(grad_scores, pair_keys)) / root
+    grad_keys = dot(grad_scores, stack, COLS_BY_COLS) / root
+    gated = (att_hat * proj_ref[:, columns(0)].astype(F32)).astype(BF16)
+    out_ref[first, :] = (ev_ref[first, :].astype(F32) + dot(gated, w_out_ref[...])).astype(BF16)
     out_ref[last, :] = out_last_ref[...]
-    grads = [
-        grad_gate,
-        grad_values[:window] + grads_ref[:, :width],
-        grad_queries,
-        grad_keys[:window] + grads_ref[:, width:],
+    own_pre = [
+        (ratio_ref[:, width:] * att_hat).astype(BF16),
+        ((grad_values[:window] + grads_ref[:, :width]) * slope_ref[:, columns(1)]).astype(BF16),
+        (grad_queries * slope_ref[:, columns(2)]).astype(BF16),
+        ((grad_keys[:window] + grads_ref[:, width:]) * slope_ref[:, columns(3)]).astype(BF16),
     ]
     tail_pre = {
         1: (grad_values[window:] * tail_values_slope).astype(BF16),
@@ -224,10 +247,9 @@
     left = jnp.concatenate([normed_ref[...], tail_normed], axis=0)
     own_total, back_total, in_blocks, bias_rows = None, None, [], []
     for i in range(4):
-        own_pre = (grads[i] * slope_ref[:, columns(i)]).astype(BF16)
-        part = dot(own_pre, w_in_ref[:, columns(i)], ROWS_BY_ROWS)
+        part = dot(own_pre[i], w_in_ref[:, columns(i)], ROWS_BY_ROWS)
         own_total = part if own_total is None else own_total + part
-        right = [own_pre, pre_ref[:, columns(i)]]
+        right = [own_pre[i], pre_ref[:, columns(i)]]
         if i in tail_pre:
             part = dot(tail_pre[i], w_in_ref[:, columns(i)], ROWS_BY_ROWS)
             back_total = part if back_total is None else back_total + part
@@ -371,16 +393,19 @@
     near, far = lax.axis_size(NEAR), lax.axis_size(FAR)
     moved = lax.ppermute(events, SEQ, [(i, i + 1) for i in range(slabs - 1)])
     half = (window, width)
-    (
-        out_last, gated, pre, own_last, normed, proj, slope, bias, grads, ev, cot, w_in_near,
-        b_in_near, w_out_near,
-    ) = call(
+    band = (heads * window, window)
+    own_last, *kept = call(
         own_kernel,
         [
-            (half, BF16), (half, BF16), ((window, 4 * width), BF16), (half, F32),
-            ((rows, width), BF16), ((window, 4 * width), BF16), ((window, 4 * width), F32),
-            ((heads * window, window), F32), ((window, 2 * width), F32), ((rows, width), BF16),
-            ((rows, width), BF16), (w_in.shape, BF16), ((1, 4 * width), F32), (w_out.shape, BF16),
+            (shape, kind, KEPT)
+            for shape, kind in [
+                (half, BF16), (half, BF16), ((window, 4 * width), BF16), (half, F32),
+                ((rows, width), BF16), ((window, 4 * width), BF16), ((window, 4 * width), F32),
+                (band, F32), (band, F32), ((window, 2 * width), F32),
+                ((heads * window, width), BF16), (half, F32), ((window, 2 * width), F32),
+                ((rows, width), BF16), ((rows, width), BF16), (w_in.shape, BF16),
+                ((1, 4 * width), F32), (w_out.shape, BF16),
+            ]
         ],
         history_lengths, events[0], cotangent[0], bucket_ids[0], w_in, b_in[None], w_out,
         pos_table, time_table,
@@ -393,12 +418,12 @@
         ],
         flops=10**9, moved=10**7,
     )
+    own_last, kept = kept[2], [own_last, *kept[:2], *kept[3:]]
+    ev, cot = kept[12:14]
     layer_out, parts, own_first = call(
         functools.partial(edge_kernel, scale),
         [((rows, width), BF16, KEPT), ((near, PIECE, 128), BF16, KEPT), (half, F32, KEPT)],
-        history_lengths, moved, out_last, gated, pre, normed, proj, slope, bias, grads, ev, cot,
-        w_in_near, b_in_near, w_out_near,
-        spaces=[pltpu.SMEM] + [pltpu.VMEM] * 14,
+        moved, *kept,
         flops=10**9, moved=10**7,
     )
     zl = lax.axis_size("zl")

time: 77.2 us -> 77.1 us (level)
  no operation moved by 1% of the time
where the time goes in v6:
time: 77.1 us; the launch traced here: 76.8 us
  blocking collectives  63.5 us (82%)
  Pallas kernels  6.96 us (9%)
  starting transfers between devices  4.51 us (6%)
  between operations  1.31 us (2%)
    all_to_all x1, blocking collectives, on_device(): parts = lax.all_to_all(parts, NEAR, 0, 0, axis_index_groups=[order])  22.6 us
    all_to_all x1, blocking collectives, on_device(): lax.all_to_all(sums, FAR, 0, 0, axis_index_groups=[[(i + 5) % far for i i...  22 us
    all_to_all x1, blocking collectives, on_device(): sums = lax.all_to_all(sums, NEAR, 0, 0, axis_index_groups=[order])  18.9 us
    pallas_call x5, Pallas kernels, call(): pl.pallas_call(kernel, out_shape=[pltpu.VMEM(shape, kind) if KEPT in plac...  6.96 us
    ppermute x1, starting transfers between devices, on_device(): moved = lax.ppermute(events, SEQ, [(i, i + 1) for i in range(slabs - 1)])  4.51 us
  transfers between devices with their start and end apart: 1, of which 1 were waited for; matrix products, arithmetic and copies ran while one was open for 0% of the time, Pallas kernels for 5%

profile of v6, /device:TPU:1, one launch (start us, length us, event | category | flops | bytes accessed | tf_op | source)
XLA Modules:
  0.0 76.8 jit_solution(4895486350248478590)
XLA Ops:
  0.6 4.5 %collective-permute-start = (bf16[1,256,256]{2,1,0:T(8,128)(2,1)}, bf16[1,256,256]{2,1,0:T(8,128)(2,1)S(1)}, u32[]{:S(2)}, u32[]{:S(2)}) collective-permute-start(bf16[1,256,256]{2,1,0:T(8,128)(2,1)} %param.9), channel_id=1, source_target_pairs={{0,1},{1,2},{2,3},{3,4},{4,5},{5,6},{6,7},{7,8},{8,9},{9,10},{10,1... | collective-permute-start | bytes 393224 | tf_op jit(solution)/shard_map/ppermute | solution.py:394
  5.8 3.5 %shard_map.128 = (bf16[128,256]{1,0:T(8,128)(2,1)S(1)}, bf16[128,256]{1,0:T(8,128)(2,1)S(1)}, bf16[128,1024]{1,0:T(8,128)(2,1)S(1)}, f32[128,256]{1,0:T(8,128)S(...) custom-call(s32[1]{0:T(128)S(6)} %copy.14.length_ref, ...), custom_call_target="tpu_custom_call" | custom-call | flops 1000000000 | bytes 10000000 | tf_op jit(solution)/shard_map/pallas_call | solution.py:369
  9.3 0.6 collective-permute-done.moved_ref
  9.8 1.9 %shard_map.129 = (bf16[256,256]{1,0:T(8,128)(2,1)S(1)}, bf16[64,48,128]{2,1,0:T(8,128)(2,1)S(1)}, f32[128,256]{1,0:T(8,128)S(1)}) custom-call(bf16[1,256,256]{2,1,0:T(8,128)(2,1)S(1)} %collective-permute-done.moved_ref, bf16[128,256]{1,0:T(8,128)(2,1)S(1)} %get-tuple-element.33.out_last_ref, bf16[128,256]{1,0:T(8,128)(2,1)S(1)} %get-tuple-element.34.gated_ref, ...), custom_call_target="tpu_custom_call" | custom-call | flops 1000000000 | bytes 10000000 | tf_op jit(solution)/shard_map/pallas_call | solution.py:369
  11.7 22.6 %all_to_all.15.parts_ref = bf16[64,48,128]{2,1,0:T(8,128)(2,1)S(1)} all-to-all(bf16[64,48,128]{2,1,0:T(8,128)(2,1)S(1)} %get-tuple-element.50), channel_id=1, replica_groups={{12,28,13,29,14,30,15,31,256,272,257,273,258,274,259,275,260,276,261,27..., dimensions={0} | all-to-all | bytes 1572864 | tf_op jit(solution)/shard_map/all_to_all | solution.py:434
  34.3 0.1 shard_map.130
  34.4 22.0 %all_to_all.16.parts_ref = bf16[8,48,128]{2,1,0:T(8,128)(2,1)S(1)} all-to-all(bf16[8,48,128]{2,1,0:T(8,128)(2,1)S(1)} %get-tuple-element.51), channel_id=1, replica_groups={{160,192,224,0,32,64,96,128},{161,193,225,1,33,65,97,129},{162,194,226,..., dimensions={0} | all-to-all | bytes 196608 | tf_op jit(solution)/shard_map/all_to_all | solution.py:438
  56.5 0.1 shard_map.131
  56.5 18.9 %all_to_all.17.all_ref = bf16[64,48,128]{2,1,0:T(8,128)(2,1)S(1)} all-to-all(bf16[64,48,128]{2,1,0:T(8,128)(2,1)S(1)} %shard_map.131), channel_id=1, replica_groups={{12,28,13,29,14,30,15,31,256,272,257,273,258,274,259,275,260,276,261,27..., dimensions={0} | all-to-all | bytes 1572864 | tf_op jit(solution)/shard_map/all_to_all | solution.py:444
  75.4 1.4 %shard_map.132 = (f32[256,1024]{1,0:T(8,128)}, f32[8,128]{1,0:T(8,128)}, f32[256,256]{1,0:T(8,128)}, bf16[256,256]{1,0:T(8,128)(2,1)}, bf16[256,256]{1,0:T(8,128)(2,1)}) custom-call(bf16[64,48,128]{2,1,0:T(8,128)(2,1)S(1)} %all_to_all.17.all_ref, f32[128,256]{1,0:T(8,128)S(1)} %get-tuple-element.53.own_first_ref, ...), custom_call_target="tpu_custom_call" | custom-call | tf_op jit(solution)/shard_map/pallas_call | solution.py:369
Async XLA Ops:
  0.6 9.2 %collective-permute-start = (bf16[1,256,256]{2,1,0:T(8,128)(2,1)}, bf16[1,256,256]{2,1,0:T(8,128)(2,1)S(1)}, u32[]{:S(2)}, u32[]{:S(2)}) collective-permute-start(bf16[1,256,256]{2,1,0:T(8,128)(2,1)} %param.9), channel_id=1, source_target_pairs={{0,1},{1,2},{2,3},{3,4},{4,5},{5,6},{6,7},{7,8},{8,9},{9,10},{10,1... | collective-permute-start | bytes 393224 | tf_op jit(solution)/shard_map/ppermute | solution.py:394

commit v7 on v6

--- a/solution.py
+++ b/solution.py
@@ -19,7 +19,7 @@
 PIECE = 6 * GROUP
 BACK = 4
 PARTS = 4
-NEAR_FIRST = 24
+NEAR_FIRST = 56
 KEPT = pltpu.VMEM
 SENT = pltpu.HBM
 

time: 77.1 us -> 76.6 us (level)
    all_to_all x1, blocking collectives: 18.9 us -> 20.3 us  [on_device(): sums = lax.all_to_all(sums, NEAR, 0, 0, axis_index_groups=[order])]
    all_to_all x1, blocking collectives: 22 us -> 20.9 us  [on_device(): lax.all_to_all(sums, FAR, 0, 0, axis_index_groups=[[(i + 5) % far for i i...]
where the time goes in v7:
time: 76.6 us; the launch traced here: 76.3 us
  blocking collectives  63 us (82%)
  Pallas kernels  6.96 us (9%)
  starting transfers between devices  4.51 us (6%)
  between operations  1.31 us (2%)
    all_to_all x1, blocking collectives, on_device(): parts = lax.all_to_all(parts, NEAR, 0, 0, axis_index_groups=[order])  21.9 us
    all_to_all x1, blocking collectives, on_device(): lax.all_to_all(sums, FAR, 0, 0, axis_index_groups=[[(i + 5) % far for i i...  20.9 us
    all_to_all x1, blocking collectives, on_device(): sums = lax.all_to_all(sums, NEAR, 0, 0, axis_index_groups=[order])  20.3 us
    pallas_call x5, Pallas kernels, call(): pl.pallas_call(kernel, out_shape=[pltpu.VMEM(shape, kind) if KEPT in plac...  6.96 us
    ppermute x1, starting transfers between devices, on_device(): moved = lax.ppermute(events, SEQ, [(i, i + 1) for i in range(slabs - 1)])  4.51 us
  transfers between devices with their start and end apart: 1, of which 1 were waited for; matrix products, arithmetic and copies ran while one was open for 0% of the time, Pallas kernels for 5%

profile of v7, /device:TPU:1, one launch (start us, length us, event | category | flops | bytes accessed | tf_op | source)
XLA Modules:
  0.0 76.3 jit_solution(10599508574177500414)
XLA Ops:
  0.6 4.5 %collective-permute-start = (bf16[1,256,256]{2,1,0:T(8,128)(2,1)}, bf16[1,256,256]{2,1,0:T(8,128)(2,1)S(1)}, u32[]{:S(2)}, u32[]{:S(2)}) collective-permute-start(bf16[1,256,256]{2,1,0:T(8,128)(2,1)} %param.9), channel_id=1, source_target_pairs={{0,1},{1,2},{2,3},{3,4},{4,5},{5,6},{6,7},{7,8},{8,9},{9,10},{10,1... | collective-permute-start | bytes 393224 | tf_op jit(solution)/shard_map/ppermute | solution.py:394
  5.8 3.5 %shard_map.128 = (bf16[128,256]{1,0:T(8,128)(2,1)S(1)}, bf16[128,256]{1,0:T(8,128)(2,1)S(1)}, bf16[128,1024]{1,0:T(8,128)(2,1)S(1)}, f32[128,256]{1,0:T(8,128)S(...) custom-call(s32[1]{0:T(128)S(6)} %copy.14.length_ref, ...), custom_call_target="tpu_custom_call" | custom-call | flops 1000000000 | bytes 10000000 | tf_op jit(solution)/shard_map/pallas_call | solution.py:369
  9.3 0.6 collective-permute-done.moved_ref
  9.8 1.9 %shard_map.129 = (bf16[256,256]{1,0:T(8,128)(2,1)S(1)}, bf16[64,48,128]{2,1,0:T(8,128)(2,1)S(1)}, f32[128,256]{1,0:T(8,128)S(1)}) custom-call(bf16[1,256,256]{2,1,0:T(8,128)(2,1)S(1)} %collective-permute-done.moved_ref, bf16[128,256]{1,0:T(8,128)(2,1)S(1)} %get-tuple-element.33.out_last_ref, bf16[128,256]{1,0:T(8,128)(2,1)S(1)} %get-tuple-element.34.gated_ref, ...), custom_call_target="tpu_custom_call" | custom-call | flops 1000000000 | bytes 10000000 | tf_op jit(solution)/shard_map/pallas_call | solution.py:369
  11.7 21.9 %all_to_all.15.parts_ref = bf16[64,48,128]{2,1,0:T(8,128)(2,1)S(1)} all-to-all(bf16[64,48,128]{2,1,0:T(8,128)(2,1)S(1)} %get-tuple-element.50), channel_id=1, replica_groups={{268,284,269,285,270,286,271,287,0,16,1,17,2,18,3,19,4,20,5,21,6,22,7,2..., dimensions={0} | all-to-all | bytes 1572864 | tf_op jit(solution)/shard_map/all_to_all | solution.py:434
  33.6 0.1 shard_map.130
  33.7 20.9 %all_to_all.16.parts_ref = bf16[8,48,128]{2,1,0:T(8,128)(2,1)S(1)} all-to-all(bf16[8,48,128]{2,1,0:T(8,128)(2,1)S(1)} %get-tuple-element.51), channel_id=1, replica_groups={{160,192,224,0,32,64,96,128},{161,193,225,1,33,65,97,129},{162,194,226,..., dimensions={0} | all-to-all | bytes 196608 | tf_op jit(solution)/shard_map/all_to_all | solution.py:438
  54.6 0.1 shard_map.131
  54.7 20.3 %all_to_all.17.all_ref = bf16[64,48,128]{2,1,0:T(8,128)(2,1)S(1)} all-to-all(bf16[64,48,128]{2,1,0:T(8,128)(2,1)S(1)} %shard_map.131), channel_id=1, replica_groups={{268,284,269,285,270,286,271,287,0,16,1,17,2,18,3,19,4,20,5,21,6,22,7,2..., dimensions={0} | all-to-all | bytes 1572864 | tf_op jit(solution)/shard_map/all_to_all | solution.py:444
  74.9 1.4 %shard_map.132 = (f32[256,1024]{1,0:T(8,128)}, f32[8,128]{1,0:T(8,128)}, f32[256,256]{1,0:T(8,128)}, bf16[256,256]{1,0:T(8,128)(2,1)}, bf16[256,256]{1,0:T(8,128)(2,1)}) custom-call(bf16[64,48,128]{2,1,0:T(8,128)(2,1)S(1)} %all_to_all.17.all_ref, f32[128,256]{1,0:T(8,128)S(1)} %get-tuple-element.53.own_first_ref, ...), custom_call_target="tpu_custom_call" | custom-call | tf_op jit(solution)/shard_map/pallas_call | solution.py:369
Async XLA Ops:
  0.6 9.2 %collective-permute-start = (bf16[1,256,256]{2,1,0:T(8,128)(2,1)}, bf16[1,256,256]{2,1,0:T(8,128)(2,1)S(1)}, u32[]{:S(2)}, u32[]{:S(2)}) collective-permute-start(bf16[1,256,256]{2,1,0:T(8,128)(2,1)} %param.9), channel_id=1, source_target_pairs={{0,1},{1,2},{2,3},{3,4},{4,5},{5,6},{6,7},{7,8},{8,9},{9,10},{10,1... | collective-permute-start | bytes 393224 | tf_op jit(solution)/shard_map/ppermute | solution.py:394

commit v8 on v7

--- a/solution.py
+++ b/solution.py
@@ -19,7 +19,8 @@
 PIECE = 6 * GROUP
 BACK = 4
 PARTS = 4
-NEAR_FIRST = 56
+FIRST_OUT = 50
+FIRST_BACK = 58
 KEPT = pltpu.VMEM
 SENT = pltpu.HBM
 
@@ -306,7 +307,7 @@
 
 
 def unpack_kernel(
-    all_ref, own_first_ref, own_last_ref, ev_ref, cot_ref, out_ref,
+    places, all_ref, own_first_ref, own_last_ref, ev_ref, cot_ref, out_ref,
     w_in_hbm, b_in_hbm, w_out_hbm, grad_hbm, out_hbm,
     w_in_ref, b_in_ref, w_out_ref, grad_ref, sems,
 ):
@@ -323,7 +324,7 @@
     pieces = all_ref.shape[0]
     part = pieces // PARTS
     for piece in range(pieces):
-        rows = all_ref[piece].astype(F32)
+        rows = all_ref[places[piece]].astype(F32)
         group, half = piece // 2, piece % 2
         here = slice(group * GROUP, (group + 1) * GROUP)
         tiles = [rows[k * GROUP : (k + 1) * GROUP] for k in range(6)]
@@ -427,9 +428,11 @@
         flops=10**9, moved=10**7,
     )
     zl = lax.axis_size("zl")
-    order = [(i + NEAR_FIRST) % near for i in range(near)]
+    order = [(i + FIRST_OUT) % near for i in range(near)]
+    back_order = [(i + FIRST_BACK) % near for i in range(near)]
+    places = [back_order.index(i) for i in order]
     sources = [
-        order.index(i + zl) if i // zl % slabs < slabs - 1 else None for i in order
+        order.index(i + zl) if i // zl % slabs < slabs - 1 else None for i in back_order
     ]
     parts = lax.all_to_all(parts, NEAR, 0, 0, axis_index_groups=[order])
     sums, back = call(
@@ -441,9 +444,9 @@
     (sums,) = call(
         functools.partial(far_kernel, sources), [((near, PIECE, 128), BF16, KEPT)], sums, back
     )
-    sums = lax.all_to_all(sums, NEAR, 0, 0, axis_index_groups=[order])
+    sums = lax.all_to_all(sums, NEAR, 0, 0, axis_index_groups=[back_order])
     sum_in, sum_bias, sum_out, grad_events, layer_out = call(
-        unpack_kernel,
+        functools.partial(unpack_kernel, places),
         [
             ((width, 4 * width), F32, SENT), ((8, 128), F32, SENT), ((width, width), F32, SENT),
             ((rows, width), BF16, SENT), ((rows, width), BF16, SENT),

time: 76.6 us -> 76 us (level)
    all_to_all x1, blocking collectives: 20.3 us -> 18.7 us  [on_device(): sums = lax.all_to_all(sums, NEAR, 0, 0, axis_index_groups=[back_order])]
where the time goes in v8:
time: 76 us; the launch traced here: 75.8 us
  blocking collectives  62.4 us (82%)
  Pallas kernels  6.96 us (9%)
  starting transfers between devices  4.51 us (6%)
  between operations  1.31 us (2%)
    all_to_all x1, blocking collectives, on_device(): parts = lax.all_to_all(parts, NEAR, 0, 0, axis_index_groups=[order])  22.2 us
    all_to_all x1, blocking collectives, on_device(): lax.all_to_all(sums, FAR, 0, 0, axis_index_groups=[[(i + 5) % far for i i...  21.5 us
    all_to_all x1, blocking collectives, on_device(): sums = lax.all_to_all(sums, NEAR, 0, 0, axis_index_groups=[back_order])  18.7 us
    pallas_call x5, Pallas kernels, call(): pl.pallas_call(kernel, out_shape=[pltpu.VMEM(shape, kind) if KEPT in plac...  6.96 us
    ppermute x1, starting transfers between devices, on_device(): moved = lax.ppermute(events, SEQ, [(i, i + 1) for i in range(slabs - 1)])  4.51 us
  transfers between devices with their start and end apart: 1, of which 1 were waited for; matrix products, arithmetic and copies ran while one was open for 0% of the time, Pallas kernels for 5%

profile of v8, /device:TPU:1, one launch (start us, length us, event | category | flops | bytes accessed | tf_op | source)
XLA Modules:
  0.0 75.8 jit_solution(11397409968681114804)
XLA Ops:
  0.6 4.5 %collective-permute-start = (bf16[1,256,256]{2,1,0:T(8,128)(2,1)}, bf16[1,256,256]{2,1,0:T(8,128)(2,1)S(1)}, u32[]{:S(2)}, u32[]{:S(2)}) collective-permute-start(bf16[1,256,256]{2,1,0:T(8,128)(2,1)} %param.9), channel_id=1, source_target_pairs={{0,1},{1,2},{2,3},{3,4},{4,5},{5,6},{6,7},{7,8},{8,9},{9,10},{10,1... | collective-permute-start | bytes 393224 | tf_op jit(solution)/shard_map/ppermute | solution.py:395
  5.8 3.5 %shard_map.128 = (bf16[128,256]{1,0:T(8,128)(2,1)S(1)}, bf16[128,256]{1,0:T(8,128)(2,1)S(1)}, bf16[128,1024]{1,0:T(8,128)(2,1)S(1)}, f32[128,256]{1,0:T(8,128)S(...) custom-call(s32[1]{0:T(128)S(6)} %copy.14.length_ref, ...), custom_call_target="tpu_custom_call" | custom-call | flops 1000000000 | bytes 10000000 | tf_op jit(solution)/shard_map/pallas_call | solution.py:370
  9.3 0.6 collective-permute-done.moved_ref
  9.8 1.9 %shard_map.129 = (bf16[256,256]{1,0:T(8,128)(2,1)S(1)}, bf16[64,48,128]{2,1,0:T(8,128)(2,1)S(1)}, f32[128,256]{1,0:T(8,128)S(1)}) custom-call(bf16[1,256,256]{2,1,0:T(8,128)(2,1)S(1)} %collective-permute-done.moved_ref, bf16[128,256]{1,0:T(8,128)(2,1)S(1)} %get-tuple-element.33.out_last_ref, bf16[128,256]{1,0:T(8,128)(2,1)S(1)} %get-tuple-element.34.gated_ref, ...), custom_call_target="tpu_custom_call" | custom-call | flops 1000000000 | bytes 10000000 | tf_op jit(solution)/shard_map/pallas_call | solution.py:370
  11.7 22.2 %all_to_all.15.parts_ref = bf16[64,48,128]{2,1,0:T(8,128)(2,1)S(1)} all-to-all(bf16[64,48,128]{2,1,0:T(8,128)(2,1)S(1)} %get-tuple-element.50), channel_id=1, replica_groups={{265,281,266,282,267,283,268,284,269,285,270,286,271,287,0,16,1,17,2,18..., dimensions={0} | all-to-all | bytes 1572864 | tf_op jit(solution)/shard_map/all_to_all | solution.py:437
  34.0 0.1 shard_map.130
  34.1 21.5 %all_to_all.16.parts_ref = bf16[8,48,128]{2,1,0:T(8,128)(2,1)S(1)} all-to-all(bf16[8,48,128]{2,1,0:T(8,128)(2,1)S(1)} %get-tuple-element.51), channel_id=1, replica_groups={{160,192,224,0,32,64,96,128},{161,193,225,1,33,65,97,129},{162,194,226,..., dimensions={0} | all-to-all | bytes 196608 | tf_op jit(solution)/shard_map/all_to_all | solution.py:441
  55.6 0.1 shard_map.131
  55.7 18.7 %all_to_all.17.all_ref = bf16[64,48,128]{2,1,0:T(8,128)(2,1)S(1)} all-to-all(bf16[64,48,128]{2,1,0:T(8,128)(2,1)S(1)} %shard_map.131), channel_id=1, replica_groups={{269,285,270,286,271,287,0,16,1,17,2,18,3,19,4,20,5,21,6,22,7,23,8,24,9..., dimensions={0} | all-to-all | bytes 1572864 | tf_op jit(solution)/shard_map/all_to_all | solution.py:447
  74.4 1.4 %shard_map.132 = (f32[256,1024]{1,0:T(8,128)}, f32[8,128]{1,0:T(8,128)}, f32[256,256]{1,0:T(8,128)}, bf16[256,256]{1,0:T(8,128)(2,1)}, bf16[256,256]{1,0:T(8,128)(2,1)}) custom-call(bf16[64,48,128]{2,1,0:T(8,128)(2,1)S(1)} %all_to_all.17.all_ref, f32[128,256]{1,0:T(8,128)S(1)} %get-tuple-element.53.own_first_ref, ...), custom_call_target="tpu_custom_call" | custom-call | tf_op jit(solution)/shard_map/pallas_call | solution.py:370
Async XLA Ops:
  0.6 9.2 %collective-permute-start = (bf16[1,256,256]{2,1,0:T(8,128)(2,1)}, bf16[1,256,256]{2,1,0:T(8,128)(2,1)S(1)}, u32[]{:S(2)}, u32[]{:S(2)}) collective-permute-start(bf16[1,256,256]{2,1,0:T(8,128)(2,1)} %param.9), channel_id=1, source_target_pairs={{0,1},{1,2},{2,3},{3,4},{4,5},{5,6},{6,7},{7,8},{8,9},{9,10},{10,1... | collective-permute-start | bytes 393224 | tf_op jit(solution)/shard_map/ppermute | solution.py:395

commit v9 on v8

--- a/solution.py
+++ b/solution.py
@@ -16,7 +16,7 @@
 BATCH = ("yl", "zh", "zl")
 SEQ = ("yh", "x", "c")
 GROUP = 8
-PIECE = 6 * GROUP
+PIECE = 5 * GROUP + 5
 BACK = 4
 PARTS = 4
 FIRST_OUT = 50
@@ -126,8 +126,8 @@
 def own_kernel(
     length_ref, ev_hbm, cot_hbm, ids_hbm, w_in_hbm, b_in_hbm, w_out_hbm, pos_hbm, time_hbm,
     out_ref, gated_ref, pre_ref, own_ref, normed_ref, proj_ref, slope_ref, base_ref, mask_ref,
-    grads_ref, stack_ref, att_ref, ratio_ref, ev_ref, cot_ref, w_in_ref, b_in_ref, w_out_ref,
-    ids_ref, pos_ref, time_ref, sems,
+    grads_ref, stack_ref, att_ref, ratio_ref, early_ref, ev_ref, cot_ref, w_in_ref, b_in_ref,
+    w_out_ref, ids_ref, pos_ref, time_ref, sems,
 ):
     pairs = [
         (ev_hbm, ev_ref), (w_in_hbm, w_in_ref), (b_in_hbm, b_in_ref), (ids_hbm, ids_ref),
@@ -173,6 +173,8 @@
     pre = (grads * slope[last]).astype(BF16)
     pre_ref[...] = pre
     own_ref[...] = dot(pre, w_in_ref[...], ROWS_BY_ROWS)
+    early_ref[:, : 4 * width] = dot(normed[last], pre, COLS_BY_COLS)
+    early_ref[:, 4 * width :] = dot(gated, cot_ref[last, :], COLS_BY_COLS)
 
     stack = band.by_head(queries[first])
     stack_ref[...] = stack
@@ -193,8 +195,8 @@
 
 def edge_kernel(
     scale, moved_ref, out_last_ref, gated_ref, pre_ref, normed_ref, proj_ref, slope_ref, base_ref,
-    mask_ref, grads_ref, stack_ref, att_ref, ratio_ref, ev_ref, cot_ref, w_in_ref, b_in_ref,
-    w_out_ref,
+    mask_ref, grads_ref, stack_ref, att_ref, ratio_ref, early_ref, ev_ref, cot_ref, w_in_ref,
+    b_in_ref, w_out_ref,
     out_ref, parts_ref, own_ref,
 ):
     rows, width = ev_ref.shape
@@ -245,23 +247,24 @@
         1: (grad_values[window:] * tail_values_slope).astype(BF16),
         3: (grad_keys[window:] * tail_keys_slope).astype(BF16),
     }
-    left = jnp.concatenate([normed_ref[...], tail_normed], axis=0)
+    left = jnp.concatenate([normed_ref[first, :], tail_normed], axis=0)
     own_total, back_total, in_blocks, bias_rows = None, None, [], []
     for i in range(4):
         part = dot(own_pre[i], w_in_ref[:, columns(i)], ROWS_BY_ROWS)
         own_total = part if own_total is None else own_total + part
-        right = [own_pre[i], pre_ref[:, columns(i)]]
+        right = [own_pre[i]]
         if i in tail_pre:
             part = dot(tail_pre[i], w_in_ref[:, columns(i)], ROWS_BY_ROWS)
             back_total = part if back_total is None else back_total + part
             right.append(tail_pre[i])
         right = jnp.concatenate(right, axis=0)
-        in_blocks.append(dot(left[: right.shape[0]], right, COLS_BY_COLS) * scale)
+        part = early_ref[:, columns(i)] + dot(left[: right.shape[0]], right, COLS_BY_COLS)
+        in_blocks.append(part * scale)
+        right = jnp.concatenate([right, pre_ref[:, columns(i)]], axis=0)
         bias_rows.append(jnp.sum(right.astype(F32), axis=0, keepdims=True) * scale)
     own_ref[...] = own_total
-    part_out = dot(
-        jnp.concatenate([gated, gated_ref[...]], axis=0), cot_ref[...], COLS_BY_COLS
-    ) * scale
+    part_out = early_ref[:, columns(4)] + dot(gated, cot_ref[first, :], COLS_BY_COLS)
+    part_out = part_out * scale
     tile_row = lax.broadcasted_iota(jnp.int32, (GROUP, 128), 0)
     for piece in range(parts_ref.shape[0]):
         group, half = piece // 2, piece % 2
@@ -280,30 +283,34 @@
         line = piece // 8
         bias = bias_rows[line // 2][:, line % 2 * 128 : (line % 2 + 1) * 128]
         tiles.append(jnp.where(tile_row < BACK, rest, jnp.broadcast_to(bias, (GROUP, 128))))
-        parts_ref[piece] = jnp.concatenate(tiles, axis=0).astype(BF16)
+        parts_ref[piece] = jnp.concatenate(tiles, axis=0)[:PIECE].astype(BF16)
+
+
+def whole(rows):
+    return jnp.concatenate([rows.astype(F32), jnp.zeros((6 * GROUP - PIECE, 128), F32)], axis=0)
 
 
 def near_kernel(parts_ref, sum_ref, back_ref):
     total = None
     for i in range(parts_ref.shape[0]):
-        piece = parts_ref[i].astype(F32)
+        piece = whole(parts_ref[i])
         back_ref[i] = piece[5 * GROUP :]
         total = piece if total is None else total + piece
-    sums = total.astype(BF16)
+    sums = total[:PIECE].astype(BF16)
     for i in range(sum_ref.shape[0]):
         sum_ref[i] = sums
 
 
 def far_kernel(sources, parts_ref, back_ref, sum_ref):
-    total = parts_ref[0].astype(F32)
+    total = whole(parts_ref[0])
     for i in range(1, parts_ref.shape[0]):
-        total = total + parts_ref[i].astype(F32)
+        total = total + whole(parts_ref[i])
     tile_row = lax.broadcasted_iota(jnp.int32, (GROUP, 128), 0)
     rest = total[5 * GROUP :]
     for i, source in enumerate(sources):
         back = jnp.zeros_like(rest) if source is None else back_ref[source]
         last = jnp.where(tile_row < BACK, back, rest)
-        sum_ref[i] = jnp.concatenate([total[: 5 * GROUP], last], axis=0).astype(BF16)
+        sum_ref[i] = jnp.concatenate([total[: 5 * GROUP], last], axis=0)[:PIECE].astype(BF16)
 
 
 def unpack_kernel(
@@ -324,7 +331,7 @@
     pieces = all_ref.shape[0]
     part = pieces // PARTS
     for piece in range(pieces):
-        rows = all_ref[places[piece]].astype(F32)
+        rows = whole(all_ref[places[piece]])
         group, half = piece // 2, piece % 2
         here = slice(group * GROUP, (group + 1) * GROUP)
         tiles = [rows[k * GROUP : (k + 1) * GROUP] for k in range(6)]
@@ -404,6 +411,7 @@
                 ((rows, width), BF16), ((window, 4 * width), BF16), ((window, 4 * width), F32),
                 (band, F32), (band, F32), ((window, 2 * width), F32),
                 ((heads * window, width), BF16), (half, F32), ((window, 2 * width), F32),
+                ((width, 5 * width), F32),
                 ((rows, width), BF16), ((rows, width), BF16), (w_in.shape, BF16),
                 ((1, 4 * width), F32), (w_out.shape, BF16),
             ]
@@ -420,7 +428,7 @@
         flops=10**9, moved=10**7,
     )
     own_last, kept = kept[2], [own_last, *kept[:2], *kept[3:]]
-    ev, cot = kept[12:14]
+    ev, cot = kept[13:15]
     layer_out, parts, own_first = call(
         functools.partial(edge_kernel, scale),
         [((rows, width), BF16, KEPT), ((near, PIECE, 128), BF16, KEPT), (half, F32, KEPT)],

time: 76 us -> 76.1 us (level)
  no operation moved by 1% of the time
where the time goes in v9:
time: 76.1 us; the launch traced here: 75.8 us
  blocking collectives  62.5 us (82%)
  Pallas kernels  7.01 us (9%)
  starting transfers between devices  4.51 us (6%)
  between operations  1.31 us (2%)
    all_to_all x1, blocking collectives, on_device(): parts = lax.all_to_all(parts, NEAR, 0, 0, axis_index_groups=[order])  22.3 us
    all_to_all x1, blocking collectives, on_device(): lax.all_to_all(sums, FAR, 0, 0, axis_index_groups=[[(i + 5) % far for i i...  21.5 us
    all_to_all x1, blocking collectives, on_device(): sums = lax.all_to_all(sums, NEAR, 0, 0, axis_index_groups=[back_order])  18.7 us
    pallas_call x5, Pallas kernels, call(): pl.pallas_call(kernel, out_shape=[pltpu.VMEM(shape, kind) if KEPT in plac...  7.01 us
    ppermute x1, starting transfers between devices, on_device(): moved = lax.ppermute(events, SEQ, [(i, i + 1) for i in range(slabs - 1)])  4.51 us
  transfers between devices with their start and end apart: 1, of which 1 were waited for; matrix products, arithmetic and copies ran while one was open for 0% of the time, Pallas kernels for 5%

profile of v9, /device:TPU:1, one launch (start us, length us, event | category | flops | bytes accessed | tf_op | source)
XLA Modules:
  0.0 75.8 jit_solution(17061976544872488983)
XLA Ops:
  0.6 4.5 %collective-permute-start = (bf16[1,256,256]{2,1,0:T(8,128)(2,1)}, bf16[1,256,256]{2,1,0:T(8,128)(2,1)S(1)}, u32[]{:S(2)}, u32[]{:S(2)}) collective-permute-start(bf16[1,256,256]{2,1,0:T(8,128)(2,1)} %param.9), channel_id=1, source_target_pairs={{0,1},{1,2},{2,3},{3,4},{4,5},{5,6},{6,7},{7,8},{8,9},{9,10},{10,1... | collective-permute-start | bytes 393224 | tf_op jit(solution)/shard_map/ppermute | solution.py:402
  5.8 3.6 %shard_map.128 = (bf16[128,256]{1,0:T(8,128)(2,1)S(1)}, bf16[128,256]{1,0:T(8,128)(2,1)S(1)}, bf16[128,1024]{1,0:T(8,128)(2,1)S(1)}, f32[128,256]{1,0:T(8,128)S(...) custom-call(s32[1]{0:T(128)S(6)} %copy.14.length_ref, ...), custom_call_target="tpu_custom_call" | custom-call | flops 1000000000 | bytes 10000000 | tf_op jit(solution)/shard_map/pallas_call | solution.py:377
  9.4 0.5 collective-permute-done.moved_ref
  9.8 1.8 %shard_map.129 = (bf16[256,256]{1,0:T(8,128)(2,1)S(1)}, bf16[64,45,128]{2,1,0:T(8,128)(2,1)S(1)}, f32[128,256]{1,0:T(8,128)S(1)}) custom-call(bf16[1,256,256]{2,1,0:T(8,128)(2,1)S(1)} %collective-permute-done.moved_ref, bf16[128,256]{1,0:T(8,128)(2,1)S(1)} %get-tuple-element.34.out_last_ref, bf16[128,256]{1,0:T(8,128)(2,1)S(1)} %get-tuple-element.35.gated_ref, ...), custom_call_target="tpu_custom_call" | custom-call | flops 1000000000 | bytes 10000000 | tf_op jit(solution)/shard_map/pallas_call | solution.py:377
  11.6 22.3 %all_to_all.15.parts_ref = bf16[64,45,128]{2,1,0:T(8,128)(2,1)S(1)} all-to-all(bf16[64,45,128]{2,1,0:T(8,128)(2,1)S(1)} %get-tuple-element.52), channel_id=1, replica_groups={{265,281,266,282,267,283,268,284,269,285,270,286,271,287,0,16,1,17,2,18..., dimensions={0} | all-to-all | bytes 1474560 | tf_op jit(solution)/shard_map/all_to_all | solution.py:445
  34.0 0.2 shard_map.130
  34.1 21.5 %all_to_all.16.parts_ref = bf16[8,45,128]{2,1,0:T(8,128)(2,1)S(1)} all-to-all(bf16[8,45,128]{2,1,0:T(8,128)(2,1)S(1)} %get-tuple-element.53), channel_id=1, replica_groups={{160,192,224,0,32,64,96,128},{161,193,225,1,33,65,97,129},{162,194,226,..., dimensions={0} | all-to-all | bytes 184320 | tf_op jit(solution)/shard_map/all_to_all | solution.py:449
  55.7 0.1 shard_map.131
  55.7 18.7 %all_to_all.17.all_ref = bf16[64,45,128]{2,1,0:T(8,128)(2,1)S(1)} all-to-all(bf16[64,45,128]{2,1,0:T(8,128)(2,1)S(1)} %shard_map.131), channel_id=1, replica_groups={{269,285,270,286,271,287,0,16,1,17,2,18,3,19,4,20,5,21,6,22,7,23,8,24,9..., dimensions={0} | all-to-all | bytes 1474560 | tf_op jit(solution)/shard_map/all_to_all | solution.py:455
  74.4 1.4 %shard_map.132 = (f32[256,1024]{1,0:T(8,128)}, f32[8,128]{1,0:T(8,128)}, f32[256,256]{1,0:T(8,128)}, bf16[256,256]{1,0:T(8,128)(2,1)}, bf16[256,256]{1,0:T(8,128)(2,1)}) custom-call(bf16[64,45,128]{2,1,0:T(8,128)(2,1)S(1)} %all_to_all.17.all_ref, f32[128,256]{1,0:T(8,128)S(1)} %get-tuple-element.55.own_first_ref, ...), custom_call_target="tpu_custom_call" | custom-call | tf_op jit(solution)/shard_map/pallas_call | solution.py:377
Async XLA Ops:
  0.6 9.2 %collective-permute-start = (bf16[1,256,256]{2,1,0:T(8,128)(2,1)}, bf16[1,256,256]{2,1,0:T(8,128)(2,1)S(1)}, u32[]{:S(2)}, u32[]{:S(2)}) collective-permute-start(bf16[1,256,256]{2,1,0:T(8,128)(2,1)} %param.9), channel_id=1, source_target_pairs={{0,1},{1,2},{2,3},{3,4},{4,5},{5,6},{6,7},{7,8},{8,9},{9,10},{10,1... | collective-permute-start | bytes 393224 | tf_op jit(solution)/shard_map/ppermute | solution.py:402

commit v10 on v8

--- a/solution.py
+++ b/solution.py
@@ -439,7 +439,7 @@
         near_kernel, [((far, PIECE, 128), BF16, KEPT), ((near, GROUP, 128), F32, KEPT)], parts
     )
     sums = lax.all_to_all(
-        sums, FAR, 0, 0, axis_index_groups=[[(i + 5) % far for i in range(far)]]
+        sums, FAR, 0, 0, axis_index_groups=[[5, 4, 3, 2, 1, 0, 7, 6]]
     )
     (sums,) = call(
         functools.partial(far_kernel, sources), [((near, PIECE, 128), BF16, KEPT)], sums, back

time: 76 us -> 75.9 us (level)
  no operation moved by 1% of the time
where the time goes in v10:
time: 75.9 us; the launch traced here: 75.6 us
  blocking collectives  62.3 us (82%)
  Pallas kernels  6.96 us (9%)
  starting transfers between devices  4.51 us (6%)
  between operations  1.31 us (2%)
    all_to_all x1, blocking collectives, on_device(): parts = lax.all_to_all(parts, NEAR, 0, 0, axis_index_groups=[order])  22.2 us
    all_to_all x1, blocking collectives, on_device(): lax.all_to_all(sums, FAR, 0, 0, axis_index_groups=[[5, 4, 3, 2, 1, 0, 7,...  22.1 us
    all_to_all x1, blocking collectives, on_device(): sums = lax.all_to_all(sums, NEAR, 0, 0, axis_index_groups=[back_order])  18 us
    pallas_call x5, Pallas kernels, call(): pl.pallas_call(kernel, out_shape=[pltpu.VMEM(shape, kind) if KEPT in plac...  6.96 us
    ppermute x1, starting transfers between devices, on_device(): moved = lax.ppermute(events, SEQ, [(i, i + 1) for i in range(slabs - 1)])  4.51 us
  transfers between devices with their start and end apart: 1, of which 1 were waited for; matrix products, arithmetic and copies ran while one was open for 0% of the time, Pallas kernels for 5%

profile of v10, /device:TPU:1, one launch (start us, length us, event | category | flops | bytes accessed | tf_op | source)
XLA Modules:
  0.0 75.6 jit_solution(16232724094108793244)
XLA Ops:
  0.6 4.5 %collective-permute-start = (bf16[1,256,256]{2,1,0:T(8,128)(2,1)}, bf16[1,256,256]{2,1,0:T(8,128)(2,1)S(1)}, u32[]{:S(2)}, u32[]{:S(2)}) collective-permute-start(bf16[1,256,256]{2,1,0:T(8,128)(2,1)} %param.9), channel_id=1, source_target_pairs={{0,1},{1,2},{2,3},{3,4},{4,5},{5,6},{6,7},{7,8},{8,9},{9,10},{10,1... | collective-permute-start | bytes 393224 | tf_op jit(solution)/shard_map/ppermute | solution.py:395
  5.8 3.5 %shard_map.128 = (bf16[128,256]{1,0:T(8,128)(2,1)S(1)}, bf16[128,256]{1,0:T(8,128)(2,1)S(1)}, bf16[128,1024]{1,0:T(8,128)(2,1)S(1)}, f32[128,256]{1,0:T(8,128)S(...) custom-call(s32[1]{0:T(128)S(6)} %copy.14.length_ref, ...), custom_call_target="tpu_custom_call" | custom-call | flops 1000000000 | bytes 10000000 | tf_op jit(solution)/shard_map/pallas_call | solution.py:370
  9.3 0.6 collective-permute-done.moved_ref
  9.8 1.9 %shard_map.129 = (bf16[256,256]{1,0:T(8,128)(2,1)S(1)}, bf16[64,48,128]{2,1,0:T(8,128)(2,1)S(1)}, f32[128,256]{1,0:T(8,128)S(1)}) custom-call(bf16[1,256,256]{2,1,0:T(8,128)(2,1)S(1)} %collective-permute-done.moved_ref, bf16[128,256]{1,0:T(8,128)(2,1)S(1)} %get-tuple-element.33.out_last_ref, bf16[128,256]{1,0:T(8,128)(2,1)S(1)} %get-tuple-element.34.gated_ref, ...), custom_call_target="tpu_custom_call" | custom-call | flops 1000000000 | bytes 10000000 | tf_op jit(solution)/shard_map/pallas_call | solution.py:370
  11.7 22.2 %all_to_all.15.parts_ref = bf16[64,48,128]{2,1,0:T(8,128)(2,1)S(1)} all-to-all(bf16[64,48,128]{2,1,0:T(8,128)(2,1)S(1)} %get-tuple-element.50), channel_id=1, replica_groups={{265,281,266,282,267,283,268,284,269,285,270,286,271,287,0,16,1,17,2,18..., dimensions={0} | all-to-all | bytes 1572864 | tf_op jit(solution)/shard_map/all_to_all | solution.py:437
  34.0 0.1 shard_map.130
  34.1 22.1 %all_to_all.16.parts_ref = bf16[8,48,128]{2,1,0:T(8,128)(2,1)S(1)} all-to-all(bf16[8,48,128]{2,1,0:T(8,128)(2,1)S(1)} %get-tuple-element.51), channel_id=1, replica_groups={{160,128,96,64,32,0,224,192},{161,129,97,65,33,1,225,193},{162,130,98,6..., dimensions={0} | all-to-all | bytes 196608 | tf_op jit(solution)/shard_map/all_to_all | solution.py:441
  56.2 0.1 shard_map.131
  56.2 18.0 %all_to_all.17.all_ref = bf16[64,48,128]{2,1,0:T(8,128)(2,1)S(1)} all-to-all(bf16[64,48,128]{2,1,0:T(8,128)(2,1)S(1)} %shard_map.131), channel_id=1, replica_groups={{269,285,270,286,271,287,0,16,1,17,2,18,3,19,4,20,5,21,6,22,7,23,8,24,9..., dimensions={0} | all-to-all | bytes 1572864 | tf_op jit(solution)/shard_map/all_to_all | solution.py:447
  74.2 1.4 %shard_map.132 = (f32[256,1024]{1,0:T(8,128)}, f32[8,128]{1,0:T(8,128)}, f32[256,256]{1,0:T(8,128)}, bf16[256,256]{1,0:T(8,128)(2,1)}, bf16[256,256]{1,0:T(8,128)(2,1)}) custom-call(bf16[64,48,128]{2,1,0:T(8,128)(2,1)S(1)} %all_to_all.17.all_ref, f32[128,256]{1,0:T(8,128)S(1)} %get-tuple-element.53.own_first_ref, ...), custom_call_target="tpu_custom_call" | custom-call | tf_op jit(solution)/shard_map/pallas_call | solution.py:370
Async XLA Ops:
  0.6 9.2 %collective-permute-start = (bf16[1,256,256]{2,1,0:T(8,128)(2,1)}, bf16[1,256,256]{2,1,0:T(8,128)(2,1)S(1)}, u32[]{:S(2)}, u32[]{:S(2)}) collective-permute-start(bf16[1,256,256]{2,1,0:T(8,128)(2,1)} %param.9), channel_id=1, source_target_pairs={{0,1},{1,2},{2,3},{3,4},{4,5},{5,6},{6,7},{7,8},{8,9},{9,10},{10,1... | collective-permute-start | bytes 393224 | tf_op jit(solution)/shard_map/ppermute | solution.py:395

commit v11 on v8

--- a/solution.py
+++ b/solution.py
@@ -19,7 +19,7 @@
 PIECE = 6 * GROUP
 BACK = 4
 PARTS = 4
-FIRST_OUT = 50
+FIRST_OUT = 18
 FIRST_BACK = 58
 KEPT = pltpu.VMEM
 SENT = pltpu.HBM

time: 76 us -> 75.9 us (level)
    all_to_all x1, blocking collectives: 21.5 us -> 20.4 us  [on_device(): lax.all_to_all(sums, FAR, 0, 0, axis_index_groups=[[(i + 5) % far for i i...]
    all_to_all x1, blocking collectives: 18.7 us -> 19.6 us  [on_device(): sums = lax.all_to_all(sums, NEAR, 0, 0, axis_index_groups=[back_order])]
where the time goes in v11:
time: 75.9 us; the launch traced here: 75.7 us
  blocking collectives  62.3 us (82%)
  Pallas kernels  6.96 us (9%)
  starting transfers between devices  4.51 us (6%)
  between operations  1.31 us (2%)
    all_to_all x1, blocking collectives, on_device(): parts = lax.all_to_all(parts, NEAR, 0, 0, axis_index_groups=[order])  22.3 us
    all_to_all x1, blocking collectives, on_device(): lax.all_to_all(sums, FAR, 0, 0, axis_index_groups=[[(i + 5) % far for i i...  20.4 us
    all_to_all x1, blocking collectives, on_device(): sums = lax.all_to_all(sums, NEAR, 0, 0, axis_index_groups=[back_order])  19.6 us
    pallas_call x5, Pallas kernels, call(): pl.pallas_call(kernel, out_shape=[pltpu.VMEM(shape, kind) if KEPT in plac...  6.96 us
    ppermute x1, starting transfers between devices, on_device(): moved = lax.ppermute(events, SEQ, [(i, i + 1) for i in range(slabs - 1)])  4.51 us
  transfers between devices with their start and end apart: 1, of which 1 were waited for; matrix products, arithmetic and copies ran while one was open for 0% of the time, Pallas kernels for 5%

profile of v11, /device:TPU:1, one launch (start us, length us, event | category | flops | bytes accessed | tf_op | source)
XLA Modules:
  0.0 75.7 jit_solution(335057690640850178)
XLA Ops:
  0.6 4.5 %collective-permute-start = (bf16[1,256,256]{2,1,0:T(8,128)(2,1)}, bf16[1,256,256]{2,1,0:T(8,128)(2,1)S(1)}, u32[]{:S(2)}, u32[]{:S(2)}) collective-permute-start(bf16[1,256,256]{2,1,0:T(8,128)(2,1)} %param.9), channel_id=1, source_target_pairs={{0,1},{1,2},{2,3},{3,4},{4,5},{5,6},{6,7},{7,8},{8,9},{9,10},{10,1... | collective-permute-start | bytes 393224 | tf_op jit(solution)/shard_map/ppermute | solution.py:395
  5.8 3.5 %shard_map.128 = (bf16[128,256]{1,0:T(8,128)(2,1)S(1)}, bf16[128,256]{1,0:T(8,128)(2,1)S(1)}, bf16[128,1024]{1,0:T(8,128)(2,1)S(1)}, f32[128,256]{1,0:T(8,128)S(...) custom-call(s32[1]{0:T(128)S(6)} %copy.14.length_ref, ...), custom_call_target="tpu_custom_call" | custom-call | flops 1000000000 | bytes 10000000 | tf_op jit(solution)/shard_map/pallas_call | solution.py:370
  9.3 0.6 collective-permute-done.moved_ref
  9.8 1.9 %shard_map.129 = (bf16[256,256]{1,0:T(8,128)(2,1)S(1)}, bf16[64,48,128]{2,1,0:T(8,128)(2,1)S(1)}, f32[128,256]{1,0:T(8,128)S(1)}) custom-call(bf16[1,256,256]{2,1,0:T(8,128)(2,1)S(1)} %collective-permute-done.moved_ref, bf16[128,256]{1,0:T(8,128)(2,1)S(1)} %get-tuple-element.33.out_last_ref, bf16[128,256]{1,0:T(8,128)(2,1)S(1)} %get-tuple-element.34.gated_ref, ...), custom_call_target="tpu_custom_call" | custom-call | flops 1000000000 | bytes 10000000 | tf_op jit(solution)/shard_map/pallas_call | solution.py:370
  11.7 22.3 %all_to_all.15.parts_ref = bf16[64,48,128]{2,1,0:T(8,128)(2,1)S(1)} all-to-all(bf16[64,48,128]{2,1,0:T(8,128)(2,1)S(1)} %get-tuple-element.50), channel_id=1, replica_groups={{9,25,10,26,11,27,12,28,13,29,14,30,15,31,256,272,257,273,258,274,259,2..., dimensions={0} | all-to-all | bytes 1572864 | tf_op jit(solution)/shard_map/all_to_all | solution.py:437
  34.1 0.1 shard_map.130
  34.2 20.4 %all_to_all.16.parts_ref = bf16[8,48,128]{2,1,0:T(8,128)(2,1)S(1)} all-to-all(bf16[8,48,128]{2,1,0:T(8,128)(2,1)S(1)} %get-tuple-element.51), channel_id=1, replica_groups={{160,192,224,0,32,64,96,128},{161,193,225,1,33,65,97,129},{162,194,226,..., dimensions={0} | all-to-all | bytes 196608 | tf_op jit(solution)/shard_map/all_to_all | solution.py:441
  54.6 0.1 shard_map.131
  54.7 19.6 %all_to_all.17.all_ref = bf16[64,48,128]{2,1,0:T(8,128)(2,1)S(1)} all-to-all(bf16[64,48,128]{2,1,0:T(8,128)(2,1)S(1)} %shard_map.131), channel_id=1, replica_groups={{269,285,270,286,271,287,0,16,1,17,2,18,3,19,4,20,5,21,6,22,7,23,8,24,9..., dimensions={0} | all-to-all | bytes 1572864 | tf_op jit(solution)/shard_map/all_to_all | solution.py:447
  74.3 1.4 %shard_map.132 = (f32[256,1024]{1,0:T(8,128)}, f32[8,128]{1,0:T(8,128)}, f32[256,256]{1,0:T(8,128)}, bf16[256,256]{1,0:T(8,128)(2,1)}, bf16[256,256]{1,0:T(8,128)(2,1)}) custom-call(bf16[64,48,128]{2,1,0:T(8,128)(2,1)S(1)} %all_to_all.17.all_ref, f32[128,256]{1,0:T(8,128)S(1)} %get-tuple-element.53.own_first_ref, ...), custom_call_target="tpu_custom_call" | custom-call | tf_op jit(solution)/shard_map/pallas_call | solution.py:370
Async XLA Ops:
  0.6 9.2 %collective-permute-start = (bf16[1,256,256]{2,1,0:T(8,128)(2,1)}, bf16[1,256,256]{2,1,0:T(8,128)(2,1)S(1)}, u32[]{:S(2)}, u32[]{:S(2)}) collective-permute-start(bf16[1,256,256]{2,1,0:T(8,128)(2,1)} %param.9), channel_id=1, source_target_pairs={{0,1},{1,2},{2,3},{3,4},{4,5},{5,6},{6,7},{7,8},{8,9},{9,10},{10,1... | collective-permute-start | bytes 393224 | tf_op jit(solution)/shard_map/ppermute | solution.py:395
